TPU v7x, 512 devices: a whole 4x8x8 slice. The times are simulated.
512 devices in a mesh: dp: 128 (over y, z_hi, x), head: 4 (over z_lo, core).
Axes of the slice: x: 4, y: 8, z: 8 (z_hi: 4, z_lo: 2; z = z_hi * 2 + z_lo), core: 2. Of those that a mesh axis runs over, the one named last changes fastest.
Arguments:
- trunk: bfloat16 [22528, 4096], P(('dp', 'head')), may hold values from -6 to 6
- keys: bfloat16 [4, 22528, 4096], P('head', 'dp'), may hold values from -900 to 900
- gains: float32 [4, 4096], P('head'), may hold values from 0.1 to 1.9
- grad_out: bfloat16 [4, 22528, 4096], P('head', 'dp'), may hold values from -6 to 6
Outputs:
- grad_trunk: bfloat16 [22528, 4096], P(('dp', 'head'))
- grad_keys: bfloat16 [4, 22528, 4096], P('head', 'dp')
- grad_gains: float32 [4, 4096], P('head')
All inputs are finite; a program needn't handle non-finite values.
Results may differ from a plain program's by a relative error of at most 0.012.
The roundings to bfloat16 on the way count: a program that leaves them out, or rounds other values in their place, can miss the bound.
Values may be sent and summed in bfloat16 or wider, within the bound.
No kernel may reach another device: no remote copies, remote signals or barrier semaphores. Data moves between devices by JAX's collectives and lax.ppermute only.
A program may use at most 64 MiB of HBM per device.

v0:
```python
import jax
import jax.numpy as jnp
from jax import lax
from jax.sharding import PartitionSpec as P

NH = 32
HEAD_DIM = 128


def norm_rows(rows):
    xf = rows.astype(jnp.float32)
    rscale = lax.rsqrt(jnp.mean(xf * xf, axis=-1, keepdims=True) + 1e-05)
    return (xf * rscale, rscale)


def on_device(trunk, keys, gains, grad_out):
    whole = lax.all_gather(trunk, "head", axis=0, tiled=True)
    length, width = whole.shape
    scale = jnp.float32(HEAD_DIM ** (-0.5))
    normed, rscale = norm_rows(whole)
    gain = gains[0]
    queries = (normed * gain).astype(jnp.bfloat16).reshape(length, NH, HEAD_DIM)
    keyset = keys[0].reshape(length, NH, HEAD_DIM)
    cotan = grad_out[0].reshape(length, NH, HEAD_DIM)
    scores = jnp.einsum("qhd,khd->hqk", queries, keyset, preferred_element_type=jnp.float32) * scale
    upper = jnp.arange(length)[:, None] >= jnp.arange(length)[None, :]
    scores = jnp.where(upper[None], scores, -jnp.inf)
    top = jnp.max(scores, axis=-1, keepdims=True)
    expo = jnp.exp(scores - top)
    probs = expo / jnp.sum(expo, axis=-1, keepdims=True)
    dprob = jnp.einsum("qhd,khd->hqk", cotan, queries, preferred_element_type=jnp.float32)
    delta = jnp.sum(probs * dprob, axis=-1, keepdims=True)
    dscore = (probs * (dprob - delta)).astype(jnp.bfloat16)
    pround = probs.astype(jnp.bfloat16)
    dquery = jnp.einsum("hqk,khd->qhd", dscore, keyset, preferred_element_type=jnp.float32) * scale
    dkey = jnp.einsum("hqk,qhd->khd", dscore, queries, preferred_element_type=jnp.float32) * scale
    dvalue = jnp.einsum("hqk,qhd->khd", pround, cotan, preferred_element_type=jnp.float32)
    dnorm = (dquery + dvalue).reshape(length, width)
    gain_term = jnp.sum(normed * dnorm, axis=0)
    weighted = gain * dnorm
    term = rscale * (weighted - normed * jnp.mean(weighted * normed, axis=-1, keepdims=True))
    summed = lax.psum_scatter(term, "head", scatter_dimension=0, tiled=True)
    grad_trunk = summed.astype(jnp.bfloat16)
    grad_gains = lax.psum(gain_term, "dp")
    grad_keys = dkey.reshape(1, length, width).astype(jnp.bfloat16)
    return (grad_trunk, grad_keys, grad_gains.reshape(1, width))


def solution(mesh):
    return jax.shard_map(
        on_device,
        mesh=mesh,
        in_specs=(
            P(("dp", "head"), None),
            P("head", "dp", None),
            P("head", None),
            P("head", "dp", None),
        ),
        out_specs=(P(("dp", "head"), None), P("head", "dp", None), P("head", None)),
        check_vma=False,
    )
```

profile of v0, /device:TPU:64, one launch (start us, length us, event | category | flops | bytes accessed | tf_op | source)
XLA Modules:
  0.0 862.6 jit_solution(4514066805027971478)
XLA Ops:
  7.2 0.0 all-gather.3.cloned.1.call-start
  7.2 0.7 all-gather.3.cloned.1.call-update
  7.9 2.8 copy.38
  10.7 0.0 copy-done.5
  10.7 1.4 copy.39
  12.1 1.3 dynamic-slice.4
  14.1 0.0 copy-start.7
  14.1 28.6 %all-gather.3.cloned.1.call-done = bf16[4,44,4096]{2,1,0:T(8,128)(2,1)} async-done(((bf16[1,44,4096]{2,1,0:T(8,128)(2,1)}), bf16[4,44,4096]{2,1,0:T(8,128)(2,1)}) %all-gather.3.cloned.1.call-update) | async-done | bytes 1441808 | tf_op jit(solution)/shard_map/all_gather | solution.py:17
  42.7 1.5 reshape.61
  44.2 0.3 multiply_reduce_fusion.1
  44.5 0.0 copy-done.7
  44.5 0.5 fusion.15
  45.0 0.9 copy-done
  45.9 1.0 fusion.19
  46.9 1.8 fusion.31
  48.7 4.1 fusion.2
  52.8 4.4 fusion.4
  57.1 1.3 fusion.23
  58.4 0.3 copy-done.1
  58.7 1.2 add_bitcast_fusion
  59.9 1.0 fusion.6
  60.9 2.2 subtract_multiply_fusion
  63.2 33.9 %fusion = f32[48,4096]{1,0:T(8,128)} fusion(f32[176,4096]{1,0:T(8,128)} %subtract_multiply_fusion), kind=kCustom, calls=%all-reduce-scatter | all-reduce-scatter fusion | flops 786433 | bytes 3672064
  97.1 1.0 slice
  98.1 2.1 collective-permute-start
  100.2 2.3 fusion.14
  102.5 0.4 copy.34
  102.8 1.5 convert_element_type.39
  104.4 747.3 %psum.7 = f32[1,4096]{1,0:T(1,128)} all-reduce(f32[1,4096]{1,0:T(1,128)S(1)} %bitcast.58), channel_id=1, replica_groups=mesh['dp'=128,'head'=4] {'dp'}, use_global_device_ids=true, to_apply=%region_7.8 | all-reduce | flops 4096 | bytes 32768 | tf_op jit(solution)/shard_map/psum | solution.py:44
  851.7 0.0 collective-permute-done
  851.7 3.2 concatenate
  854.9 0.8 dynamic-slice_convert_fusion
  (14 shorter events, 0.1 us)
Async XLA Ops:
  7.2 3.5 copy-start.5
  7.2 35.5 %all-gather.3.cloned.1.call-start = ((), (), s32[]{:S(2)}) async-start(), calls=%async_computation | async-start | bytes 1966080 | tf_op jit(solution)/shard_map/all_gather | solution.py:17
  14.1 30.5 %copy-start.7 = (f32[1,4096]{1,0:T(1,128)S(1)}, f32[1,4096]{1,0:T(1,128)}, u32[]{:S(2)}) copy-start(f32[1,4096]{1,0:T(1,128)} %param.6) | copy-start | bytes 49156
  44.5 1.4 copy-start
  45.0 3.7 copy-start.3
  46.8 1.8 copy-start.6
  57.1 1.6 copy-start.1
  63.1 37.0 %copy-start.2 = (bf16[32,176,176]{1,2,0:T(8,128)(2,1)S(1)}, bf16[32,176,176]{1,2,0:T(8,128)(2,1)}, u32[]{:S(2)}) copy-start(bf16[32,176,176]{1,2,0:T(8,128)(2,1)} %copy-done.1) | copy-start | bytes 5947396
  98.1 753.6 %collective-permute-start = (bf16[12,4096]{1,0:T(8,128)(2,1)S(1)}, bf16[12,4096]{1,0:T(8,128)(2,1)S(1)}, u32[]{:S(2)}, u32[]{:S(2)}) collective-permute-start(bf16[12,4096]{1,0:T(8,128)(2,1)S(1)} %slice), channel_id=1, source_target_pairs={{0,1},{1,2},{2,3},{4,5},{5,6},{6,7},{8,9},{9,10},{10,11},{12,13},{... | collective-permute-start | bytes 294920
  102.5 749.2 %copy-start.4 = (f32[48,4096]{1,0:T(8,128)S(1)}, f32[48,4096]{1,0:T(8,128)}, u32[]{:S(2)}) copy-start(f32[48,4096]{1,0:T(8,128)} %fusion) | copy-start | bytes 2359300
Sparse Core Ops, SparseCore 0:
  10.1 32.5 all-gather.2
where the time goes:
time: 863 us
  blocking collectives  781 us (90%)
  waiting for transfers between devices  29.3 us (3%)
  local copies, waits for them, and re-layouts  15.1 us (2%)
  between operations  14.9 us (2%)
  other arithmetic  10.2 us (1%)
  matrix products  9.82 us (1%)
    psum x1, blocking collectives, on_device(): grad_gains = lax.psum(gain_term, 'dp')  747 us
    unnamed x1, blocking collectives  33.9 us
    all_gather x1, waiting for transfers between devices, on_device(): whole = lax.all_gather(trunk, 'head', axis=0, tiled=True)  28.6 us
  transfers between devices with their start and end apart: 2, of which 1 were waited for; matrix products, arithmetic and copies ran while one was open for 1% of the time, Pallas kernels for 0%

commit v1 on v0

v1 whole, which is shorter than its diff:
```python
import functools
import math

import jax
import jax.numpy as jnp
from jax import lax
from jax.experimental import pallas as pl
from jax.experimental.pallas import tpu as pltpu
from jax.sharding import Mesh
from jax.sharding import PartitionSpec as P

NH = 32
HEAD_DIM = 128
BF = jnp.bfloat16
F32 = jnp.float32
NT = (((1,), (1,)), ((), ()))
TN = (((0,), (0,)), ((), ()))
HEAD = ("zl", "core")
LIMIT = 48 * 1024 * 1024


def attention_kernel(peers, own, core, far, farcore, keys_hbm, cot_hbm, gain_ref, gk_ref, give_ref, keep_ref, gterm_ref,
                     xf, w, rs, macc, gsum, keys, cot, sems):
    part = own.shape[0]
    length, width = xf.shape
    fetch_k = pltpu.make_async_copy(keys_hbm.at[0], keys, sems.at[0])
    fetch_g = pltpu.make_async_copy(cot_hbm.at[0], cot, sems.at[1])
    fetch_k.start()
    fetch_g.start()
    zl = lax.axis_index("zl")
    c = lax.axis_index("core")

    def columns(a):
        return pl.ds(pl.multiple_of(a * HEAD_DIM, HEAD_DIM), HEAD_DIM)

    for zi in range(2):
        for ci in range(2):

            @pl.when((zl == zi) & (c == ci))
            def _(zi=zi, ci=ci):
                here = 2 * part * zi
                there = 2 * part * (1 - zi)
                for ref, base, which in ((own, here, ci), (core, here, 1 - ci), (far, there, ci), (farcore, there, 1 - ci)):
                    start = base + part * which

                    def put(a, _, ref=ref, start=start):
                        sl = columns(a)
                        xf[pl.ds(start, part), sl] = ref[:, sl].astype(F32)
                        return 0

                    lax.fori_loop(0, width // HEAD_DIM, put, 0, unroll=4)

    def square(a, acc):
        v = xf[:, columns(a)]
        return acc + v * v

    total = lax.fori_loop(0, width // HEAD_DIM, square, jnp.zeros((length, HEAD_DIM), F32), unroll=2)
    mean = jnp.sum(total, axis=-1, keepdims=True) * (1.0 / width)
    rs[...] = jnp.broadcast_to(lax.rsqrt(mean + 1e-05), rs.shape)
    macc[...] = jnp.zeros_like(macc)
    fetch_k.wait()
    fetch_g.wait()
    scale = F32(HEAD_DIM ** (-0.5))
    scale2 = F32(HEAD_DIM ** (-0.5) * math.log2(math.e))

    def head(a, _):
        sl = columns(a)
        normed = xf[:, sl] * rs[...]
        gain = gain_ref[:, sl]
        q = (normed * gain).astype(BF)
        k = keys[:, sl]
        g = cot[:, sl]
        st = lax.dot_general(k, q, NT, preferred_element_type=F32)
        dpt = lax.dot_general(q, g, NT, preferred_element_type=F32)
        cols = lax.broadcasted_iota(jnp.int32, st.shape, 1)
        rows = lax.broadcasted_iota(jnp.int32, st.shape, 0)
        st = jnp.where(rows <= cols, st, -jnp.inf)
        top = jnp.max(st, axis=0, keepdims=True)
        e = jnp.exp2((st - top) * scale2)
        p = e * (1.0 / jnp.sum(e, axis=0, keepdims=True))
        pd = p * dpt
        delta = jnp.sum(pd, axis=0, keepdims=True)
        dst = (pd - p * delta).astype(BF)
        pb = p.astype(BF)
        dv = jnp.dot(pb, g, preferred_element_type=F32)
        dk = jnp.dot(dst, q, preferred_element_type=F32)
        dq = lax.dot_general(dst, k, TN, preferred_element_type=F32)
        gk_ref[0, :, sl] = (dk * scale).astype(BF)
        dn = dq * scale + dv
        nd = normed * dn
        gsum[pl.ds(a, 1), :] = jnp.sum(nd, axis=0, keepdims=True)
        macc[...] += nd * gain
        w[:, sl] = gain * dn
        return 0

    lax.fori_loop(0, NH, head, 0)
    for i in range(peers):
        gterm_ref[i] = gsum[...].astype(BF)
    r = rs[...]
    m = jnp.sum(macc[...], axis=-1, keepdims=True) * (1.0 / width)
    macc[...] = r * r * m
    for ci in range(2):

        @pl.when(c == ci)
        def _(ci=ci):
            def finish(a, _):
                sl = columns(a)
                term = rs[...] * w[:, sl] - macc[...] * xf[:, sl]
                for zi in range(2):
                    mine = part * (2 * zi + ci)
                    other = part * (2 * zi + 1 - ci)
                    keep_ref[zi, :, sl] = term[mine : mine + part]
                    give_ref[zi, :, sl] = term[other : other + part].astype(BF)
                return 0

            lax.fori_loop(0, width // HEAD_DIM, finish, 0)


def add_kernel(keep, got, mine_ref, send_ref):
    zl = lax.axis_index("zl")
    mine_ref[...] = keep[zl] + got[zl].astype(F32)
    send_ref[...] = (keep[1 - zl] + got[1 - zl].astype(F32)).astype(BF)


def final_kernel(mine, got, out):
    out[...] = (mine[...] + got[...].astype(F32)).astype(BF)


def spread_kernel(peers, got, out):
    total = jnp.sum(got[...].astype(F32), axis=0).astype(BF)
    for i in range(peers):
        out[i] = total


def total_kernel(got, out):
    total = jnp.sum(got[...].astype(F32), axis=0)
    for r in range(total.shape[0]):
        out[0:1, r * HEAD_DIM : (r + 1) * HEAD_DIM] = total[r : r + 1, :]


def swap(v, bit):
    return lax.ppermute(v, HEAD, [(i, i ^ bit) for i in range(4)])


def call(kernel, outs, *args, name, **more):
    return pl.pallas_call(
        kernel,
        out_shape=outs,
        in_specs=[pl.BlockSpec(memory_space=pltpu.VMEM)] * len(args),
        out_specs=jax.tree.map(lambda _: pl.BlockSpec(memory_space=pltpu.VMEM), outs),
        compiler_params=pltpu.CompilerParams(vmem_limit_bytes=LIMIT),
        name=name,
        **more,
    )(*args)


def on_device(near, rest, trunk, keys, gains, grad_out):
    part, width = trunk.shape
    length = keys.shape[1]
    shape = jax.ShapeDtypeStruct
    far = swap(trunk, 2)
    core = swap(trunk, 1)
    farcore = swap(far, 1)
    vmem = pl.BlockSpec(memory_space=pltpu.VMEM)
    hbm = pl.BlockSpec(memory_space=pl.ANY)
    grad_keys, give, keep, gterm = pl.pallas_call(
        functools.partial(attention_kernel, near),
        out_shape=(
            shape((1, length, width), BF),
            shape((2, part, width), BF),
            shape((2, part, width), F32),
            shape((near, NH, HEAD_DIM), BF),
        ),
        in_specs=[vmem] * 4 + [hbm] * 2 + [vmem],
        out_specs=(vmem,) * 4,
        scratch_shapes=[
            pltpu.VMEM((length, width), F32),
            pltpu.VMEM((length, width), F32),
            pltpu.VMEM((length, HEAD_DIM), F32),
            pltpu.VMEM((length, HEAD_DIM), F32),
            pltpu.VMEM((NH, HEAD_DIM), F32),
            pltpu.VMEM((length, width), BF),
            pltpu.VMEM((length, width), BF),
            pltpu.SemaphoreType.DMA((2,)),
        ],
        compiler_params=pltpu.CompilerParams(vmem_limit_bytes=LIMIT),
        name="attention_backward",
    )(trunk, core, far, farcore, keys, grad_out, gains)
    got = swap(give, 1)
    first = lax.all_to_all(gterm, "x", 0, 0, tiled=True)
    mine, send = call(add_kernel, (shape((part, width), F32), shape((part, width), BF)), keep, got, name="add_core")
    last = swap(send, 2)
    wide = call(functools.partial(spread_kernel, rest), shape((rest, NH, HEAD_DIM), BF), first, name="sum_near")
    second = lax.all_to_all(wide, ("y", "zh"), 0, 0, tiled=True)
    grad_trunk = call(final_kernel, shape((part, width), BF), mine, last, name="add_far")
    grad_gains = call(total_kernel, shape((1, width), F32), second, name="sum_rest")
    return grad_trunk, grad_keys, grad_gains


def solution(mesh):
    dp = mesh.shape["dp"]
    near = min(dp, 4)
    zh = 4 if dp >= 16 else 1
    y = dp // near // zh
    fine = Mesh(mesh.devices.reshape(y, zh, near, 2, 2), ("y", "zh", "x", "zl", "core"))
    dps = ("y", "zh", "x")
    return jax.shard_map(
        functools.partial(on_device, near, dp // near),
        mesh=fine,
        in_specs=(
            P(dps + HEAD, None),
            P(HEAD, dps, None),
            P(HEAD, None),
            P(HEAD, dps, None),
        ),
        out_specs=(P(dps + HEAD, None), P(HEAD, dps, None), P(HEAD, None)),
        check_vma=False,
    )
```

time: 863 us -> 91.7 us (0.11)
  the two profiles are of different devices: /device:TPU:64 before, /device:TPU:1 now
where the time goes in v1:
time: 91.7 us; the launch traced here: 91.2 us
  starting transfers between devices  39.1 us (43%)
  Pallas kernels  24.5 us (27%)
  waiting for transfers between devices  14.6 us (16%)
  blocking collectives  6.65 us (7%)
  local copies, waits for them, and re-layouts  5.58 us (6%)
    ppermute x5, starting transfers between devices, swap(): return lax.ppermute(v, HEAD, [(i, i ^ bit) for i in range(4)])  24.2 us
    pallas_call x1, Pallas kernels, on_device(): pl.pallas_call(functools.partial(attention_kernel, near), out_shape=(shap...  22.2 us
    all_to_all x1, starting transfers between devices, on_device(): second = lax.all_to_all(wide, ('y', 'zh'), 0, 0, tiled=True)  14.8 us
    all_to_all x1, waiting for transfers between devices, on_device(): second = lax.all_to_all(wide, ('y', 'zh'), 0, 0, tiled=True)  8.19 us
    all_to_all x1, blocking collectives, on_device(): first = lax.all_to_all(gterm, 'x', 0, 0, tiled=True)  6.65 us
    ppermute x5, waiting for transfers between devices, swap(): return lax.ppermute(v, HEAD, [(i, i ^ bit) for i in range(4)])  6.38 us
    unnamed x10, local copies, waits for them, and re-layouts  4.44 us
    pallas_call x4, Pallas kernels, call(): pl.pallas_call(kernel, out_shape=outs, in_specs=[pl.BlockSpec(memory_spac...  2.35 us
  transfers between devices with their start and end apart: 6, of which 3 were waited for; matrix products, arithmetic and copies ran while one was open for 0% of the time, Pallas kernels for 2%

profile of v1, /device:TPU:1, one launch (start us, length us, event | category | flops | bytes accessed | tf_op | source)
XLA Modules:
  0.0 91.2 jit_solution(5697542562771283411)
XLA Ops:
  0.6 4.8 %collective-permute-start.1 = (bf16[44,4096]{1,0:T(8,128)(2,1)}, bf16[44,4096]{1,0:T(8,128)(2,1)S(1)}, u32[]{:S(2)}, u32[]{:S(2)}) collective-permute-start(bf16[44,4096]{1,0:T(8,128)(2,1)} %own.1), channel_id=1, source_target_pairs={{0,2},{1,3},{2,0},{3,1},{4,6},{5,7},{6,4},{7,5},{8,10},{9,11},{10,... | collective-permute-start | bytes 1081352 | tf_op jit(solution)/shard_map/ppermute | solution.py:142
  5.5 5.9 %collective-permute-start = (bf16[44,4096]{1,0:T(8,128)(2,1)}, bf16[44,4096]{1,0:T(8,128)(2,1)S(1)}, u32[]{:S(2)}, u32[]{:S(2)}) collective-permute-start(bf16[44,4096]{1,0:T(8,128)(2,1)} %own.1), channel_id=1, source_target_pairs={{0,1},{1,0},{2,3},{3,2},{4,5},{5,4},{6,7},{7,6},{8,9},{9,8},{10,11... | collective-permute-start | bytes 1081352 | tf_op jit(solution)/shard_map/ppermute | solution.py:142
  11.4 0.0 collective-permute-done.1.far
  11.4 7.9 %collective-permute-start.2 = (bf16[44,4096]{1,0:T(8,128)(2,1)S(1)}, bf16[44,4096]{1,0:T(8,128)(2,1)S(1)}, u32[]{:S(2)}, u32[]{:S(2)}) collective-permute-start(bf16[44,4096]{1,0:T(8,128)(2,1)S(1)} %collective-permute-done.1.far), channel_id=1, source_target_pairs={{0,1},{1,0},{2,3},{3,2},{4,5},{5,4},{6,7},{7,6},{8,9},{9,8},{10,11... | collective-permute-start | bytes 1081352 | tf_op jit(solution)/shard_map/ppermute | solution.py:142
  19.3 0.0 collective-permute-done.core
  19.3 1.3 %collective-permute-done.2.farcore = bf16[44,4096]{1,0:T(8,128)(2,1)S(1)} collective-permute-done((bf16[44,4096]{1,0:T(8,128)(2,1)S(1)}, bf16[44,4096]{1,0:T(8,128)(2,1)S(1)}, u32[]{:S(2)}, u32[]{:S(2)}) %collective-permute-start.2) | collective-permute-done | bytes 360480 | tf_op jit(solution)/shard_map/ppermute | solution.py:142
  20.6 0.0 copy-start.1
  20.6 1.4 %copy-done.1 = bf16[1,176,4096]{2,1,0:T(8,128)(2,1)S(1)} copy-done((bf16[1,176,4096]{2,1,0:T(8,128)(2,1)S(1)}, bf16[1,176,4096]{2,1,0:T(8,128)(2,1)}, u32[]{:S(2)}) %copy-start.1) | copy-done | bytes 1441816
  22.0 0.0 copy-start.2
  22.0 1.4 %copy-done.2 = bf16[1,176,4096]{2,1,0:T(8,128)(2,1)S(1)} copy-done((bf16[1,176,4096]{2,1,0:T(8,128)(2,1)S(1)}, bf16[1,176,4096]{2,1,0:T(8,128)(2,1)}, u32[]{:S(2)}) %copy-start.2) | copy-done | bytes 1441816
  23.3 0.0 copy-start.3
  23.3 1.0 %copy-done.3 = bf16[44,4096]{1,0:T(8,128)(2,1)S(1)} copy-done((bf16[44,4096]{1,0:T(8,128)(2,1)S(1)}, bf16[44,4096]{1,0:T(8,128)(2,1)}, u32[]{:S(2)}) %copy-start.3) | copy-done | bytes 360472
  24.3 0.0 copy-start.4
  24.3 0.7 copy-done.4
  25.1 22.2 %attention_backward.1 = (bf16[1,176,4096]{2,1,0:T(8,128)(2,1)}, bf16[2,44,4096]{2,1,0:T(8,128)(2,1)S(1)}, f32[2,44,4096]{2,1,0:T(8,128)}, bf16[4,32,128]{2,1,0:T(8,128)(2,1)S(1)}) custom-call(bf16[44,4096]{1,0:T(8,128)(2,1)S(1)} %copy-done.3, bf16[44,4096]{1,0:T(8,128)(2,1)S(1)} %collective-permute-done.core, ...), custom_call_target="tpu_custom_call" | custom-call | tf_op jit(solution)/shard_map/attention_backward/pallas_call | solution.py:166
  47.3 0.7 copy.7
  48.0 0.0 copy-start
  48.0 2.5 %collective-permute-start.3 = (bf16[2,44,4096]{2,0,1:T(2,128)(2,1)S(1)}, bf16[2,44,4096]{2,0,1:T(2,128)(2,1)S(1)}, u32[]{:S(2)}, u32[]{:S(2)}) collective-permute-start(bf16[2,44,4096]{2,0,1:T(2,128)(2,1)S(1)} %copy.7), channel_id=1, source_target_pairs={{0,1},{1,0},{2,3},{3,2},{4,5},{5,4},{6,7},{7,6},{8,9},{9,8},{10,11... | collective-permute-start | bytes 2162696 | tf_op jit(solution)/shard_map/ppermute | solution.py:142
  50.5 6.7 %all_to_all.10.got = bf16[4,32,128]{2,1,0:T(8,128)(2,1)S(1)} all-to-all(bf16[4,32,128]{2,1,0:T(8,128)(2,1)S(1)} %get-tuple-element.14), channel_id=1, replica_groups=mesh['y'=8,'zh'=4,'x'=4,'zl'=2,'core'=2] {'x'}, dimensions={0} | all-to-all | bytes 65536 | tf_op jit(solution)/shard_map/all_to_all | solution.py:190
  57.2 0.7 sum_near.1
  57.9 14.8 %all-to-all-start.1 = ((bf16[32,32,128]{2,1,0:T(8,128)(2,1)}), bf16[32,32,128]{2,1,0:T(8,128)(2,1)S(1)}, u32[]{:S(2)}, u32[]{:S(2)}) async-start(bf16[32,32,128]{2,1,0:T(8,128)(2,1)} %sum_near.1), calls=%async_computation.1 | async-start | bytes 524288 | tf_op jit(solution)/shard_map/all_to_all | solution.py:194
  72.7 0.0 collective-permute-done.3
  72.8 0.4 copy.8.got
  73.2 0.0 copy-done
  73.2 0.1 add_core.1
  73.3 3.1 %collective-permute-start.4 = (bf16[44,4096]{1,0:T(8,128)(2,1)S(1)}, bf16[44,4096]{1,0:T(8,128)(2,1)S(1)}, u32[]{:S(2)}, u32[]{:S(2)}) collective-permute-start(bf16[44,4096]{1,0:T(8,128)(2,1)S(1)} %get-tuple-element.12), channel_id=1, source_target_pairs={{0,2},{1,3},{2,0},{3,1},{4,6},{5,7},{6,4},{7,5},{8,10},{9,11},{10,... | collective-permute-start | bytes 1081352 | tf_op jit(solution)/shard_map/ppermute | solution.py:142
  76.4 8.2 %all-to-all-done.1.got = bf16[32,32,128]{2,1,0:T(8,128)(2,1)S(1)} async-done(((bf16[32,32,128]{2,1,0:T(8,128)(2,1)}), bf16[32,32,128]{2,1,0:T(8,128)(2,1)S(1)}, u32[]{:S(2)}, u32[]{:S(2)}) %all-to-all-start.1) | async-done | bytes 262176 | tf_op jit(solution)/shard_map/all_to_all | solution.py:194
  84.6 0.7 sum_rest.1
  85.3 5.1 %collective-permute-done.4.got = bf16[44,4096]{1,0:T(8,128)(2,1)S(1)} collective-permute-done((bf16[44,4096]{1,0:T(8,128)(2,1)S(1)}, bf16[44,4096]{1,0:T(8,128)(2,1)S(1)}, u32[]{:S(2)}, u32[]{:S(2)}) %collective-permute-start.4) | collective-permute-done | bytes 360480 | tf_op jit(solution)/shard_map/ppermute | solution.py:142
  90.4 0.8 add_far.1
Async XLA Ops:
  0.6 10.7 %collective-permute-start.1 = (bf16[44,4096]{1,0:T(8,128)(2,1)}, bf16[44,4096]{1,0:T(8,128)(2,1)S(1)}, u32[]{:S(2)}, u32[]{:S(2)}) collective-permute-start(bf16[44,4096]{1,0:T(8,128)(2,1)} %own.1), channel_id=1, source_target_pairs={{0,2},{1,3},{2,0},{3,1},{4,6},{5,7},{6,4},{7,5},{8,10},{9,11},{10,... | collective-permute-start | bytes 1081352 | tf_op jit(solution)/shard_map/ppermute | solution.py:142
  5.5 13.8 %collective-permute-start = (bf16[44,4096]{1,0:T(8,128)(2,1)}, bf16[44,4096]{1,0:T(8,128)(2,1)S(1)}, u32[]{:S(2)}, u32[]{:S(2)}) collective-permute-start(bf16[44,4096]{1,0:T(8,128)(2,1)} %own.1), channel_id=1, source_target_pairs={{0,1},{1,0},{2,3},{3,2},{4,5},{5,4},{6,7},{7,6},{8,9},{9,8},{10,11... | collective-permute-start | bytes 1081352 | tf_op jit(solution)/shard_map/ppermute | solution.py:142
  11.4 9.3 %collective-permute-start.2 = (bf16[44,4096]{1,0:T(8,128)(2,1)S(1)}, bf16[44,4096]{1,0:T(8,128)(2,1)S(1)}, u32[]{:S(2)}, u32[]{:S(2)}) collective-permute-start(bf16[44,4096]{1,0:T(8,128)(2,1)S(1)} %collective-permute-done.1.far), channel_id=1, source_target_pairs={{0,1},{1,0},{2,3},{3,2},{4,5},{5,4},{6,7},{7,6},{8,9},{9,8},{10,11... | collective-permute-start | bytes 1081352 | tf_op jit(solution)/shard_map/ppermute | solution.py:142
  20.6 1.4 %copy-start.1 = (bf16[1,176,4096]{2,1,0:T(8,128)(2,1)S(1)}, bf16[1,176,4096]{2,1,0:T(8,128)(2,1)}, u32[]{:S(2)}) copy-start(bf16[1,176,4096]{2,1,0:T(8,128)(2,1)} %keys_hbm.1) | copy-start | bytes 4325380
  22.0 1.4 %copy-start.2 = (bf16[1,176,4096]{2,1,0:T(8,128)(2,1)S(1)}, bf16[1,176,4096]{2,1,0:T(8,128)(2,1)}, u32[]{:S(2)}) copy-start(bf16[1,176,4096]{2,1,0:T(8,128)(2,1)} %cot_hbm.1) | copy-start | bytes 4325380
  23.3 1.0 %copy-start.3 = (bf16[44,4096]{1,0:T(8,128)(2,1)S(1)}, bf16[44,4096]{1,0:T(8,128)(2,1)}, u32[]{:S(2)}) copy-start(bf16[44,4096]{1,0:T(8,128)(2,1)} %own.1) | copy-start | bytes 1081348
  24.3 0.7 copy-start.4
  48.0 25.2 %copy-start = (f32[2,44,4096]{2,1,0:T(8,128)S(1)}, f32[2,44,4096]{2,1,0:T(8,128)}, u32[]{:S(2)}) copy-start(f32[2,44,4096]{2,1,0:T(8,128)} %get-tuple-element.9.keep) | copy-start | bytes 4325380
  48.0 24.7 %collective-permute-start.3 = (bf16[2,44,4096]{2,0,1:T(2,128)(2,1)S(1)}, bf16[2,44,4096]{2,0,1:T(2,128)(2,1)S(1)}, u32[]{:S(2)}, u32[]{:S(2)}) collective-permute-start(bf16[2,44,4096]{2,0,1:T(2,128)(2,1)S(1)} %copy.7), channel_id=1, source_target_pairs={{0,1},{1,0},{2,3},{3,2},{4,5},{5,4},{6,7},{7,6},{8,9},{9,8},{10,11... | collective-permute-start | bytes 2162696 | tf_op jit(solution)/shard_map/ppermute | solution.py:142
  57.9 26.7 %all-to-all-start.1 = ((bf16[32,32,128]{2,1,0:T(8,128)(2,1)}), bf16[32,32,128]{2,1,0:T(8,128)(2,1)S(1)}, u32[]{:S(2)}, u32[]{:S(2)}) async-start(bf16[32,32,128]{2,1,0:T(8,128)(2,1)} %sum_near.1), calls=%async_computation.1 | async-start | bytes 524288 | tf_op jit(solution)/shard_map/all_to_all | solution.py:194
  73.3 17.0 %collective-permute-start.4 = (bf16[44,4096]{1,0:T(8,128)(2,1)S(1)}, bf16[44,4096]{1,0:T(8,128)(2,1)S(1)}, u32[]{:S(2)}, u32[]{:S(2)}) collective-permute-start(bf16[44,4096]{1,0:T(8,128)(2,1)S(1)} %get-tuple-element.12), channel_id=1, source_target_pairs={{0,2},{1,3},{2,0},{3,1},{4,6},{5,7},{6,4},{7,5},{8,10},{9,11},{10,... | collective-permute-start | bytes 1081352 | tf_op jit(solution)/shard_map/ppermute | solution.py:142

commit v2 on v1

v2 whole, which is shorter than its diff:
```python
import functools
import math

import jax
import jax.numpy as jnp
from jax import lax
from jax.experimental import pallas as pl
from jax.experimental.pallas import tpu as pltpu
from jax.sharding import Mesh
from jax.sharding import PartitionSpec as P

NH = 32
HEAD_DIM = 128
GROUP = 8
SLAB = 48
BF = jnp.bfloat16
F32 = jnp.float32
NT = (((1,), (1,)), ((), ()))
TN = (((0,), (0,)), ((), ()))
HEAD = ("zl", "core")
LIMIT = 24 * 1024 * 1024


def columns(a):
    return pl.ds(pl.multiple_of(a * HEAD_DIM, HEAD_DIM), HEAD_DIM)


def pair_rows(c, first, second, x_ref, rs_ref, base):
    part, width = first.shape
    for ci in range(2):

        @pl.when(c == ci)
        def _(ci=ci):
            low, high = (first, second) if ci == 0 else (second, first)

            def put(a, acc):
                sl = columns(a)
                v = jnp.concatenate([low[:, sl].astype(F32), high[:, sl].astype(F32)], axis=0)
                x_ref[pl.ds(base, 2 * part), sl] = v
                return acc + v * v

            total = lax.fori_loop(0, width // HEAD_DIM, put, jnp.zeros((2 * part, HEAD_DIM), F32), unroll=4)
            mean = jnp.sum(total, axis=-1, keepdims=True) * (1.0 / width)
            rs_ref[pl.ds(base, 2 * part), :] = jnp.broadcast_to(lax.rsqrt(mean + 1e-05), (2 * part, HEAD_DIM))


def near_kernel(own, core, keys, cot, gain, x_ref, rs_ref):
    pair_rows(lax.axis_index("core"), own, core, x_ref, rs_ref, 0)


def attention_kernel(peers, near, near_rs, far, farcore, keys, cot, gain_ref, gk_ref, give_ref, keep_ref, gterm_ref,
                     xf, w, rs, macc, gsum, bias0, bias1, gk, gsems):
    part = far.shape[0]
    length, width = xf.shape
    zl = lax.axis_index("zl")
    c = lax.axis_index("core")
    here = pl.multiple_of(2 * part * zl, 8)
    there = pl.multiple_of(2 * part * (1 - zl), 8)
    pair_rows(c, far, farcore, xf, rs, there)

    def place(a, _):
        sl = columns(a)
        xf[pl.ds(here, 2 * part), sl] = near[:, sl]
        return 0

    lax.fori_loop(0, width // HEAD_DIM, place, 0, unroll=4)
    rs[pl.ds(here, 2 * part), :] = near_rs[...]
    macc[...] = jnp.zeros_like(macc)
    scale = F32(HEAD_DIM ** (-0.5))
    scale2 = F32(HEAD_DIM ** (-0.5) * math.log2(math.e))
    cut = HEAD_DIM
    tail = length - cut

    def triangle(n):
        rows = lax.broadcasted_iota(jnp.int32, (n, n), 0)
        cols = lax.broadcasted_iota(jnp.int32, (n, n), 1)
        return jnp.where(rows <= cols, F32(0), F32(-jnp.inf))

    bias0[...] = triangle(cut)
    bias1[...] = triangle(tail)

    def softmax(s, d):
        top = jnp.max(s, axis=0, keepdims=True)
        e = jnp.exp2(s * scale2 - top * scale2)
        inv = 1.0 / jnp.sum(e, axis=0, keepdims=True)
        delta = jnp.sum(e * d, axis=0, keepdims=True) * inv
        p = e * inv
        return p.astype(BF), (p * (d - delta)).astype(BF)

    def begin(a):
        sl = columns(a)
        normed = xf[:, sl] * rs[...]
        q = (normed * gain_ref[:, sl]).astype(BF)
        st = lax.dot_general(keys[0, :, sl], q, NT, preferred_element_type=F32)
        dpt = lax.dot_general(q, cot[0, :, sl], NT, preferred_element_type=F32)
        return sl, q, st, dpt

    def middle(sl, q, st, dpt):
        p0, d0 = softmax(st[:cut, :cut] + bias0[...], dpt[:cut, :cut])
        s1 = jnp.concatenate([st[:cut, cut:], st[cut:, cut:] + bias1[...]], axis=0)
        p1, d1 = softmax(s1, dpt[:, cut:])
        none = jnp.zeros((tail, cut), BF)
        pb = jnp.concatenate([jnp.concatenate([p0, none], axis=0), p1], axis=1)
        dst = jnp.concatenate([jnp.concatenate([d0, none], axis=0), d1], axis=1)
        return sl, q, pb, dst

    def end(a, sl, q, pb, dst):
        dv = jnp.dot(pb, cot[0, :, sl], preferred_element_type=F32)
        dk = jnp.dot(dst, q, preferred_element_type=F32)
        dq = lax.dot_general(dst, keys[0, :, sl], TN, preferred_element_type=F32)
        gk[0, :, sl] = (dk * scale).astype(BF)
        dn = dq * scale + dv
        nd = xf[:, sl] * rs[...] * dn
        gain = gain_ref[:, sl]
        gsum[pl.ds(a, 1), :] = jnp.sum(nd, axis=0, keepdims=True)
        w[:, sl] = gain * dn
        return nd * gain

    def send_group(i):
        sl = pl.ds(pl.multiple_of(i * GROUP * HEAD_DIM, GROUP * HEAD_DIM), GROUP * HEAD_DIM)
        return pltpu.make_async_copy(gk.at[0, :, sl], gk_ref.at[0, :, sl], gsems.at[i])

    def heads(i, _):
        first, second, mean = {}, {}, None
        for step in range(GROUP + 2):
            if step < GROUP:
                first[step] = begin(i * GROUP + step)
            if 0 <= step - 1 < GROUP:
                second[step - 1] = middle(*first.pop(step - 1))
            if 0 <= step - 2 < GROUP:
                one = end(i * GROUP + step - 2, *second.pop(step - 2))
                mean = one if mean is None else mean + one
        macc[...] += mean
        send_group(i).start()
        return 0

    lax.fori_loop(0, NH // GROUP, heads, 0)
    for i in range(peers):
        gterm_ref[i] = gsum[...].astype(BF)
    r = rs[...]
    m = jnp.sum(macc[...], axis=-1, keepdims=True) * (1.0 / width)
    macc[...] = r * r * m
    for ci in range(2):

        @pl.when(c == ci)
        def _(ci=ci):
            def finish(a, _):
                sl = columns(a)
                term = rs[...] * w[:, sl] - macc[...] * xf[:, sl]
                for zi in range(2):
                    mine = part * (2 * zi + ci)
                    other = part * (2 * zi + 1 - ci)
                    keep_ref[SLAB * zi : SLAB * zi + part, sl] = term[mine : mine + part]
                    give_ref[SLAB * zi : SLAB * zi + part, sl] = term[other : other + part].astype(BF)
                return 0

            lax.fori_loop(0, width // HEAD_DIM, finish, 0, unroll=2)

    for i in range(NH // GROUP):
        send_group(i).wait()


def spread_kernel(peers, first, wide_ref):
    total = jnp.sum(first[...].astype(F32), axis=0).astype(BF)
    for i in range(peers):
        wide_ref[i] = total


def between_kernel(keep, got, mine_ref, send_ref):
    zl = lax.axis_index("zl")
    here = pl.ds(pl.multiple_of(SLAB * zl, SLAB), SLAB)
    there = pl.ds(pl.multiple_of(SLAB * (1 - zl), SLAB), SLAB)
    mine_ref[...] = keep[here, :] + got[here, :].astype(F32)
    send_ref[:SLAB] = (keep[there, :] + got[there, :].astype(F32)).astype(send_ref.dtype)


def final_kernel(mine, last, second, trunk_ref, gains_ref):
    total = jnp.sum(second[...].astype(F32), axis=0)
    for r in range(total.shape[0]):
        gains_ref[0:1, r * HEAD_DIM : (r + 1) * HEAD_DIM] = total[r : r + 1, :]
    both = mine[...] + last[:SLAB].astype(F32)
    trunk_ref[...] = both[: trunk_ref.shape[0]].astype(BF)


def swap(v, bit):
    return lax.ppermute(v, HEAD, [(i, i ^ bit) for i in range(4)])


def call(kernel, outs, args, name, hbm_in=(), hbm_out=(), scratch=(), cost=(0, 0), limit=LIMIT):
    vmem = pl.BlockSpec(memory_space=pltpu.VMEM)
    hbm = pl.BlockSpec(memory_space=pltpu.HBM)
    return pl.pallas_call(
        kernel,
        out_shape=outs,
        in_specs=[hbm if i in hbm_in else vmem for i in range(len(args))],
        out_specs=tuple(hbm if i in hbm_out else vmem for i in range(len(outs))),
        scratch_shapes=list(scratch),
        compiler_params=pltpu.CompilerParams(vmem_limit_bytes=limit),
        cost_estimate=pl.CostEstimate(flops=cost[0], bytes_accessed=cost[1], transcendentals=0),
        name=name,
    )(*args)


def on_device(near, rest, trunk, keys, gains, grad_out):
    part, width = trunk.shape
    length = keys.shape[1]
    shape = jax.ShapeDtypeStruct
    far = swap(trunk, 2)
    core = swap(trunk, 1)
    x_near, rs_near = call(
        near_kernel,
        (
            shape((2 * part, width), F32),
            shape((2 * part, HEAD_DIM), F32),
        ),
        (trunk, core, keys, grad_out, gains),
        "near_rows",
        cost=(0, 8 << 20),
        limit=24 * 1024 * 1024,
    )
    far, x_near = lax.optimization_barrier((far, x_near))
    farcore = swap(far, 1)
    grad_keys, give, keep, gterm = call(
        functools.partial(attention_kernel, near),
        (
            shape((1, length, width), BF),
            shape((2 * SLAB, width), BF),
            shape((2 * SLAB, width), F32),
            shape((near, NH, HEAD_DIM), BF),
        ),
        (x_near, rs_near, far, farcore, keys, grad_out, gains),
        "attention_backward",
        hbm_out=(0,),
        scratch=[
            pltpu.VMEM((length, width), F32),
            pltpu.VMEM((length, width), F32),
            pltpu.VMEM((length, HEAD_DIM), F32),
            pltpu.VMEM((length, HEAD_DIM), F32),
            pltpu.VMEM((NH, HEAD_DIM), F32),
            pltpu.VMEM((HEAD_DIM, HEAD_DIM), F32),
            pltpu.VMEM((length - HEAD_DIM, length - HEAD_DIM), F32),
            pltpu.VMEM((1, length, width), BF),
            pltpu.SemaphoreType.DMA((NH // GROUP,)),
        ],
        cost=(10 * length * length * width, 16 << 20),
    )
    got = swap(give, 1)
    first = lax.all_to_all(gterm, "zh", 0, 0, tiled=True)
    got, first = lax.optimization_barrier((got, first))
    mine, send = call(
        between_kernel, (shape((SLAB, width), F32), shape((64, width), BF)), (keep, got), "add_core"
    )
    send, first = lax.optimization_barrier((send, first))
    last = swap(send, 2)
    (wide,) = call(
        functools.partial(spread_kernel, rest),
        (shape((rest, NH, HEAD_DIM), BF),),
        (first,),
        "sum_near",
        cost=(8 << 30, 0),
    )
    second = lax.all_to_all(wide, ("y", "x"), 0, 0, tiled=True)
    grad_trunk, grad_gains = call(
        final_kernel, (shape((part, width), BF), shape((1, width), F32)), (mine, last, second), "add_far"
    )
    return grad_trunk, grad_keys, grad_gains


def solution(mesh):
    dp = mesh.shape["dp"]
    near = min(dp, 4)
    zh = 4 if dp >= 16 else 1
    y = dp // near // zh
    fine = Mesh(mesh.devices.reshape(y, zh, near, 2, 2), ("y", "zh", "x", "zl", "core"))
    dps = ("y", "zh", "x")
    return jax.shard_map(
        functools.partial(on_device, zh, dp // zh),
        mesh=fine,
        in_specs=(
            P(dps + HEAD, None),
            P(HEAD, dps, None),
            P(HEAD, None),
            P(HEAD, dps, None),
        ),
        out_specs=(P(dps + HEAD, None), P(HEAD, dps, None), P(HEAD, None)),
        check_vma=False,
    )
```

time: 91.7 us -> 73.7 us (0.80)
  the two profiles are of different devices: /device:TPU:1 before, /device:TPU:8 now
where the time goes in v2:
time: 73.7 us; the launch traced here: 73.3 us
  blocking collectives  38.4 us (52%)
  starting transfers between devices  13.4 us (18%)
  Pallas kernels  9.56 us (13%)
  waiting for transfers between devices  6.78 us (9%)
  local copies, waits for them, and re-layouts  4.44 us (6%)
    all_to_all x1, blocking collectives, on_device(): second = lax.all_to_all(wide, ('y', 'x'), 0, 0, tiled=True)  21 us
    all_to_all x1, blocking collectives, on_device(): first = lax.all_to_all(gterm, 'zh', 0, 0, tiled=True)  17.4 us
    ppermute x5, starting transfers between devices, swap(): return lax.ppermute(v, HEAD, [(i, i ^ bit) for i in range(4)])  13.4 us
    pallas_call x5, Pallas kernels, call(): pl.pallas_call(kernel, out_shape=outs, in_specs=[hbm if i in hbm_in else...  9.56 us
    ppermute x5, waiting for transfers between devices, swap(): return lax.ppermute(v, HEAD, [(i, i ^ bit) for i in range(4)])  6.78 us
    unnamed x12, local copies, waits for them, and re-layouts  4.44 us
  transfers between devices with their start and end apart: 5, of which 2 were waited for; matrix products, arithmetic and copies ran while one was open for 0% of the time, Pallas kernels for 1%

profile of v2, /device:TPU:8, one launch (start us, length us, event | category | flops | bytes accessed | tf_op | source)
XLA Modules:
  0.0 73.3 jit_solution(1810420614957289268)
XLA Ops:
  0.6 1.9 %collective-permute-start.1 = (bf16[44,4096]{1,0:T(8,128)(2,1)}, bf16[44,4096]{1,0:T(8,128)(2,1)S(1)}, u32[]{:S(2)}, u32[]{:S(2)}) collective-permute-start(bf16[44,4096]{1,0:T(8,128)(2,1)} %own.1), channel_id=1, source_target_pairs={{0,1},{1,0},{2,3},{3,2},{4,5},{5,4},{6,7},{7,6},{8,9},{9,8},{10,11... | collective-permute-start | bytes 1081352 | tf_op jit(solution)/shard_map/ppermute | solution.py:186
  2.6 4.3 %collective-permute-start = (bf16[44,4096]{1,0:T(8,128)(2,1)}, bf16[44,4096]{1,0:T(8,128)(2,1)S(1)}, u32[]{:S(2)}, u32[]{:S(2)}) collective-permute-start(bf16[44,4096]{1,0:T(8,128)(2,1)} %own.1), channel_id=1, source_target_pairs={{0,2},{1,3},{2,0},{3,1},{4,6},{5,7},{6,4},{7,5},{8,10},{9,11},{10,... | collective-permute-start | bytes 1081352 | tf_op jit(solution)/shard_map/ppermute | solution.py:186
  6.8 0.0 collective-permute-done.1.core
  6.9 0.0 copy-start
  6.9 1.4 %copy-done = bf16[1,176,4096]{2,1,0:T(8,128)(2,1)S(1)} copy-done((bf16[1,176,4096]{2,1,0:T(8,128)(2,1)S(1)}, bf16[1,176,4096]{2,1,0:T(8,128)(2,1)}, u32[]{:S(2)}) %copy-start) | copy-done | bytes 1441816
  8.2 0.0 copy-start.2
  8.2 1.4 %copy-done.2 = bf16[1,176,4096]{2,1,0:T(8,128)(2,1)S(1)} copy-done((bf16[1,176,4096]{2,1,0:T(8,128)(2,1)S(1)}, bf16[1,176,4096]{2,1,0:T(8,128)(2,1)}, u32[]{:S(2)}) %copy-start.2) | copy-done | bytes 1441816
  9.6 0.0 copy-start.4
  9.6 1.0 %copy-done.4 = bf16[44,4096]{1,0:T(8,128)(2,1)S(1)} copy-done((bf16[44,4096]{1,0:T(8,128)(2,1)S(1)}, bf16[44,4096]{1,0:T(8,128)(2,1)}, u32[]{:S(2)}) %copy-start.4) | copy-done | bytes 360472
  10.6 0.0 copy-start.5
  10.6 0.7 copy-done.5
  11.3 0.0 copy-start.1
  11.3 0.0 copy-start.3
  11.3 0.4 near_rows.1
  11.7 5.1 %collective-permute-done.far = bf16[44,4096]{1,0:T(8,128)(2,1)S(1)} collective-permute-done((bf16[44,4096]{1,0:T(8,128)(2,1)}, bf16[44,4096]{1,0:T(8,128)(2,1)S(1)}, u32[]{:S(2)}, u32[]{:S(2)}) %collective-permute-start) | collective-permute-done | bytes 360480 | tf_op jit(solution)/shard_map/ppermute | solution.py:186
  16.8 1.9 %collective-permute-start.2 = (bf16[44,4096]{1,0:T(8,128)(2,1)S(1)}, bf16[44,4096]{1,0:T(8,128)(2,1)S(1)}, u32[]{:S(2)}, u32[]{:S(2)}) collective-permute-start(bf16[44,4096]{1,0:T(8,128)(2,1)S(1)} %collective-permute-done.far), channel_id=1, source_target_pairs={{0,1},{1,0},{2,3},{3,2},{4,5},{5,4},{6,7},{7,6},{8,9},{9,8},{10,11... | collective-permute-start | bytes 1081352 | tf_op jit(solution)/shard_map/ppermute | solution.py:186
  18.7 1.7 %collective-permute-done.2.farcore = bf16[44,4096]{1,0:T(8,128)(2,1)S(1)} collective-permute-done((bf16[44,4096]{1,0:T(8,128)(2,1)S(1)}, bf16[44,4096]{1,0:T(8,128)(2,1)S(1)}, u32[]{:S(2)}, u32[]{:S(2)}) %collective-permute-start.2) | collective-permute-done | bytes 360480 | tf_op jit(solution)/shard_map/ppermute | solution.py:186
  20.4 0.0 copy-done.1
  20.4 0.0 copy-done.3
  20.4 8.1 %attention_backward.1 = (bf16[1,176,4096]{2,1,0:T(8,128)(2,1)}, bf16[96,4096]{1,0:T(8,128)(2,1)S(1)}, f32[96,4096]{1,0:T(8,128)S(1)}, bf16[4,32,128]{2,1,0:T(8,128)(2,1)S(1)}) custom-call(f32[88,4096]{1,0:T(8,128)S(1)} %get-tuple-element.20.near, f32[88,128]{1,0:T(8,128)S(1)} %get-tuple-element.21.near_rs, bf16[44,4096]{1,0:T(8,128)(2,1)S(1)} %collective-permute-done.far, ...), custom_call_target="tpu_custom_call" | custom-call | flops 1268776960 | bytes 16777216 | tf_op jit(solution)/shard_map/attention_backward/pallas_call | solution.py:192
  28.5 2.0 %collective-permute-start.3 = (bf16[96,4096]{1,0:T(8,128)(2,1)S(1)}, bf16[96,4096]{1,0:T(8,128)(2,1)S(1)}, u32[]{:S(2)}, u32[]{:S(2)}) collective-permute-start(bf16[96,4096]{1,0:T(8,128)(2,1)S(1)} %get-tuple-element.24), channel_id=1, source_target_pairs={{0,1},{1,0},{2,3},{3,2},{4,5},{5,4},{6,7},{7,6},{8,9},{9,8},{10,11... | collective-permute-start | bytes 2359304 | tf_op jit(solution)/shard_map/ppermute | solution.py:186
  30.5 17.4 %all_to_all.10.first = bf16[4,32,128]{2,1,0:T(8,128)(2,1)S(1)} all-to-all(bf16[4,32,128]{2,1,0:T(8,128)(2,1)S(1)} %get-tuple-element.25), channel_id=1, replica_groups=mesh['y'=8,'zh'=4,'x'=4,'zl'=2,'core'=2] {'zh'}, dimensions={0} | all-to-all | bytes 65536 | tf_op jit(solution)/shard_map/all_to_all | solution.py:248
  47.9 0.0 collective-permute-done.3.got
  47.9 0.1 add_core.1
  48.1 3.3 %collective-permute-start.4 = (bf16[64,4096]{1,0:T(8,128)(2,1)S(1)}, bf16[64,4096]{1,0:T(8,128)(2,1)S(1)}, u32[]{:S(2)}, u32[]{:S(2)}) collective-permute-start(bf16[64,4096]{1,0:T(8,128)(2,1)S(1)} %get-tuple-element.30), channel_id=1, source_target_pairs={{0,2},{1,3},{2,0},{3,1},{4,6},{5,7},{6,4},{7,5},{8,10},{9,11},{10,... | collective-permute-start | bytes 1572872 | tf_op jit(solution)/shard_map/ppermute | solution.py:186
  51.4 21.0 %all_to_all.11.second = bf16[32,32,128]{2,1,0:T(8,128)(2,1)S(1)} all-to-all(bf16[32,32,128]{2,1,0:T(8,128)(2,1)S(1)} %sum_near.1), channel_id=1, replica_groups=mesh['y'=8,'zh'=4,'x'=4,'zl'=2,'core'=2] {'y','x'}, dimensions={0} | all-to-all | bytes 524288 | tf_op jit(solution)/shard_map/all_to_all | solution.py:262
  72.4 0.0 collective-permute-done.4.last
  72.4 0.9 %add_far.1 = (bf16[44,4096]{1,0:T(8,128)(2,1)}, f32[1,4096]{1,0:T(1,128)}) custom-call(f32[48,4096]{1,0:T(8,128)S(1)} %get-tuple-element.27.mine, bf16[64,4096]{1,0:T(8,128)(2,1)S(1)} %collective-permute-done.4.last, bf16[32,32,128]{2,1,0:T(8,128)(2,1)S(1)} %all_to_all.11.second), custom_call_target="tpu_custom_call" | custom-call | tf_op jit(solution)/shard_map/add_far/pallas_call | solution.py:192
  (1 shorter events, 0.0 us)
Async XLA Ops:
  0.6 6.2 %collective-permute-start.1 = (bf16[44,4096]{1,0:T(8,128)(2,1)}, bf16[44,4096]{1,0:T(8,128)(2,1)S(1)}, u32[]{:S(2)}, u32[]{:S(2)}) collective-permute-start(bf16[44,4096]{1,0:T(8,128)(2,1)} %own.1), channel_id=1, source_target_pairs={{0,1},{1,0},{2,3},{3,2},{4,5},{5,4},{6,7},{7,6},{8,9},{9,8},{10,11... | collective-permute-start | bytes 1081352 | tf_op jit(solution)/shard_map/ppermute | solution.py:186
  2.6 14.3 %collective-permute-start = (bf16[44,4096]{1,0:T(8,128)(2,1)}, bf16[44,4096]{1,0:T(8,128)(2,1)S(1)}, u32[]{:S(2)}, u32[]{:S(2)}) collective-permute-start(bf16[44,4096]{1,0:T(8,128)(2,1)} %own.1), channel_id=1, source_target_pairs={{0,2},{1,3},{2,0},{3,1},{4,6},{5,7},{6,4},{7,5},{8,10},{9,11},{10,... | collective-permute-start | bytes 1081352 | tf_op jit(solution)/shard_map/ppermute | solution.py:186
  6.9 1.4 %copy-start = (bf16[1,176,4096]{2,1,0:T(8,128)(2,1)S(1)}, bf16[1,176,4096]{2,1,0:T(8,128)(2,1)}, u32[]{:S(2)}) copy-start(bf16[1,176,4096]{2,1,0:T(8,128)(2,1)} %keys.3) | copy-start | bytes 4325380
  8.2 1.4 %copy-start.2 = (bf16[1,176,4096]{2,1,0:T(8,128)(2,1)S(1)}, bf16[1,176,4096]{2,1,0:T(8,128)(2,1)}, u32[]{:S(2)}) copy-start(bf16[1,176,4096]{2,1,0:T(8,128)(2,1)} %cot.3) | copy-start | bytes 4325380
  9.6 1.0 %copy-start.4 = (bf16[44,4096]{1,0:T(8,128)(2,1)S(1)}, bf16[44,4096]{1,0:T(8,128)(2,1)}, u32[]{:S(2)}) copy-start(bf16[44,4096]{1,0:T(8,128)(2,1)} %own.1) | copy-start | bytes 1081348
  10.6 0.7 copy-start.5
  11.3 9.1 %copy-start.1 = (bf16[1,176,4096]{2,1,0:T(8,128)(2,1)S(1)}, bf16[1,176,4096]{2,1,0:T(8,128)(2,1)}, u32[]{:S(2)}) copy-start(bf16[1,176,4096]{2,1,0:T(8,128)(2,1)} %keys.3) | copy-start | bytes 4325380
  11.3 9.1 %copy-start.3 = (bf16[1,176,4096]{2,1,0:T(8,128)(2,1)S(1)}, bf16[1,176,4096]{2,1,0:T(8,128)(2,1)}, u32[]{:S(2)}) copy-start(bf16[1,176,4096]{2,1,0:T(8,128)(2,1)} %cot.3) | copy-start | bytes 4325380
  16.8 3.6 %collective-permute-start.2 = (bf16[44,4096]{1,0:T(8,128)(2,1)S(1)}, bf16[44,4096]{1,0:T(8,128)(2,1)S(1)}, u32[]{:S(2)}, u32[]{:S(2)}) collective-permute-start(bf16[44,4096]{1,0:T(8,128)(2,1)S(1)} %collective-permute-done.far), channel_id=1, source_target_pairs={{0,1},{1,0},{2,3},{3,2},{4,5},{5,4},{6,7},{7,6},{8,9},{9,8},{10,11... | collective-permute-start | bytes 1081352 | tf_op jit(solution)/shard_map/ppermute | solution.py:186
  28.5 19.4 %collective-permute-start.3 = (bf16[96,4096]{1,0:T(8,128)(2,1)S(1)}, bf16[96,4096]{1,0:T(8,128)(2,1)S(1)}, u32[]{:S(2)}, u32[]{:S(2)}) collective-permute-start(bf16[96,4096]{1,0:T(8,128)(2,1)S(1)} %get-tuple-element.24), channel_id=1, source_target_pairs={{0,1},{1,0},{2,3},{3,2},{4,5},{5,4},{6,7},{7,6},{8,9},{9,8},{10,11... | collective-permute-start | bytes 2359304 | tf_op jit(solution)/shard_map/ppermute | solution.py:186
  48.1 24.3 %collective-permute-start.4 = (bf16[64,4096]{1,0:T(8,128)(2,1)S(1)}, bf16[64,4096]{1,0:T(8,128)(2,1)S(1)}, u32[]{:S(2)}, u32[]{:S(2)}) collective-permute-start(bf16[64,4096]{1,0:T(8,128)(2,1)S(1)} %get-tuple-element.30), channel_id=1, source_target_pairs={{0,2},{1,3},{2,0},{3,1},{4,6},{5,7},{6,4},{7,5},{8,10},{9,11},{10,... | collective-permute-start | bytes 1572872 | tf_op jit(solution)/shard_map/ppermute | solution.py:186

commit v3 on v2

--- a/solution.py
+++ b/solution.py
@@ -11,7 +11,7 @@
 
 NH = 32
 HEAD_DIM = 128
-GROUP = 8
+GROUP = 16
 SLAB = 48
 BF = jnp.bfloat16
 F32 = jnp.float32
@@ -44,11 +44,21 @@
             rs_ref[pl.ds(base, 2 * part), :] = jnp.broadcast_to(lax.rsqrt(mean + 1e-05), (2 * part, HEAD_DIM))
 
 
-def near_kernel(own, core, keys, cot, gain, x_ref, rs_ref):
-    pair_rows(lax.axis_index("core"), own, core, x_ref, rs_ref, 0)
-
-
-def attention_kernel(peers, near, near_rs, far, farcore, keys, cot, gain_ref, gk_ref, give_ref, keep_ref, gterm_ref,
+def own_kernel(own, keys, cot, gain, x_ref, rs_ref):
+    part, width = own.shape
+
+    def put(a, acc):
+        sl = columns(a)
+        v = own[:, sl].astype(F32)
+        x_ref[:, sl] = v
+        return acc + v * v
+
+    total = lax.fori_loop(0, width // HEAD_DIM, put, jnp.zeros((part, HEAD_DIM), F32), unroll=4)
+    mean = jnp.sum(total, axis=-1, keepdims=True) * (1.0 / width)
+    rs_ref[...] = jnp.broadcast_to(lax.rsqrt(mean + 1e-05), (part, HEAD_DIM))
+
+
+def attention_kernel(peers, own, own_rs, core, far, farcore, keys, cot, gain_ref, gk_ref, give_ref, keep_ref, gterm_ref,
                      xf, w, rs, macc, gsum, bias0, bias1, gk, gsems):
     part = far.shape[0]
     length, width = xf.shape
@@ -57,14 +67,7 @@
     here = pl.multiple_of(2 * part * zl, 8)
     there = pl.multiple_of(2 * part * (1 - zl), 8)
     pair_rows(c, far, farcore, xf, rs, there)
-
-    def place(a, _):
-        sl = columns(a)
-        xf[pl.ds(here, 2 * part), sl] = near[:, sl]
-        return 0
-
-    lax.fori_loop(0, width // HEAD_DIM, place, 0, unroll=4)
-    rs[pl.ds(here, 2 * part), :] = near_rs[...]
+    pair_rows(c, own, core, xf, rs, here)
     macc[...] = jnp.zeros_like(macc)
     scale = F32(HEAD_DIM ** (-0.5))
     scale2 = F32(HEAD_DIM ** (-0.5) * math.log2(math.e))
@@ -207,18 +210,15 @@
     shape = jax.ShapeDtypeStruct
     far = swap(trunk, 2)
     core = swap(trunk, 1)
-    x_near, rs_near = call(
-        near_kernel,
-        (
-            shape((2 * part, width), F32),
-            shape((2 * part, HEAD_DIM), F32),
-        ),
-        (trunk, core, keys, grad_out, gains),
-        "near_rows",
+    x_own, rs_own = call(
+        own_kernel,
+        (shape((part, width), F32), shape((part, HEAD_DIM), F32)),
+        (trunk, keys, grad_out, gains),
+        "own_rows",
         cost=(0, 8 << 20),
         limit=24 * 1024 * 1024,
     )
-    far, x_near = lax.optimization_barrier((far, x_near))
+    far, x_own = lax.optimization_barrier((far, x_own))
     farcore = swap(far, 1)
     grad_keys, give, keep, gterm = call(
         functools.partial(attention_kernel, near),
@@ -228,7 +228,7 @@
             shape((2 * SLAB, width), F32),
             shape((near, NH, HEAD_DIM), BF),
         ),
-        (x_near, rs_near, far, farcore, keys, grad_out, gains),
+        (x_own, rs_own, core, far, farcore, keys, grad_out, gains),
         "attention_backward",
         hbm_out=(0,),
         scratch=[

time: 73.7 us -> 70.8 us (0.961)
  waiting for transfers between devices: 6.78 us -> 4.39 us
    ppermute x5, waiting for transfers between devices: 6.78 us -> 4.39 us  [swap(): return lax.ppermute(v, HEAD, [(i, i ^ bit) for i in range(4)])]
    unnamed x12 -> x14, local copies, waits for them, and re-layouts: 4.44 us -> 4.44 us
  transfers between devices with their start and end apart: 5 -> 5, of which waited for: 2 -> 2; matrix products, arithmetic and copies ran while one was open for 0% -> 0% of each run, Pallas kernels for 1% -> 0%
where the time goes in v3:
time: 70.8 us; the launch traced here: 70.4 us
  blocking collectives  38.4 us (54%)
  starting transfers between devices  13.4 us (19%)
  Pallas kernels  9.06 us (13%)
  local copies, waits for them, and re-layouts  4.44 us (6%)
  waiting for transfers between devices  4.39 us (6%)
  between operations  0.72 us (1%)
    all_to_all x1, blocking collectives, on_device(): second = lax.all_to_all(wide, ('y', 'x'), 0, 0, tiled=True)  21 us
    all_to_all x1, blocking collectives, on_device(): first = lax.all_to_all(gterm, 'zh', 0, 0, tiled=True)  17.4 us
    ppermute x5, starting transfers between devices, swap(): return lax.ppermute(v, HEAD, [(i, i ^ bit) for i in range(4)])  13.4 us
    pallas_call x5, Pallas kernels, call(): pl.pallas_call(kernel, out_shape=outs, in_specs=[hbm if i in hbm_in else...  9.06 us
    unnamed x14, local copies, waits for them, and re-layouts  4.44 us
    ppermute x5, waiting for transfers between devices, swap(): return lax.ppermute(v, HEAD, [(i, i ^ bit) for i in range(4)])  4.39 us
  transfers between devices with their start and end apart: 5, of which 2 were waited for; matrix products, arithmetic and copies ran while one was open for 0% of the time, Pallas kernels for 0%

profile of v3, /device:TPU:8, one launch (start us, length us, event | category | flops | bytes accessed | tf_op | source)
XLA Modules:
  0.0 70.4 jit_solution(6095018419480170323)
XLA Ops:
  0.6 4.3 %collective-permute-start = (bf16[44,4096]{1,0:T(8,128)(2,1)}, bf16[44,4096]{1,0:T(8,128)(2,1)S(1)}, u32[]{:S(2)}, u32[]{:S(2)}) collective-permute-start(bf16[44,4096]{1,0:T(8,128)(2,1)} %own.1), channel_id=1, source_target_pairs={{0,2},{1,3},{2,0},{3,1},{4,6},{5,7},{6,4},{7,5},{8,10},{9,11},{10,... | collective-permute-start | bytes 1081352 | tf_op jit(solution)/shard_map/ppermute | solution.py:189
  4.9 1.9 %collective-permute-start.1 = (bf16[44,4096]{1,0:T(8,128)(2,1)}, bf16[44,4096]{1,0:T(8,128)(2,1)S(1)}, u32[]{:S(2)}, u32[]{:S(2)}) collective-permute-start(bf16[44,4096]{1,0:T(8,128)(2,1)} %own.1), channel_id=1, source_target_pairs={{0,1},{1,0},{2,3},{3,2},{4,5},{5,4},{6,7},{7,6},{8,9},{9,8},{10,11... | collective-permute-start | bytes 1081352 | tf_op jit(solution)/shard_map/ppermute | solution.py:189
  6.8 0.0 copy-start
  6.9 1.4 %copy-done = bf16[1,176,4096]{2,1,0:T(8,128)(2,1)S(1)} copy-done((bf16[1,176,4096]{2,1,0:T(8,128)(2,1)S(1)}, bf16[1,176,4096]{2,1,0:T(8,128)(2,1)}, u32[]{:S(2)}) %copy-start) | copy-done | bytes 1441816
  8.2 0.0 copy-start.2
  8.2 1.4 %copy-done.2 = bf16[1,176,4096]{2,1,0:T(8,128)(2,1)S(1)} copy-done((bf16[1,176,4096]{2,1,0:T(8,128)(2,1)S(1)}, bf16[1,176,4096]{2,1,0:T(8,128)(2,1)}, u32[]{:S(2)}) %copy-start.2) | copy-done | bytes 1441816
  9.6 0.0 copy-start.4
  9.6 1.0 %copy-done.4 = bf16[44,4096]{1,0:T(8,128)(2,1)S(1)} copy-done((bf16[44,4096]{1,0:T(8,128)(2,1)S(1)}, bf16[44,4096]{1,0:T(8,128)(2,1)}, u32[]{:S(2)}) %copy-start.4) | copy-done | bytes 360472
  10.6 0.0 copy-start.5
  10.6 0.7 %copy-done.5 = f32[1,4096]{1,0:T(1,128)S(1)} copy-done((f32[1,4096]{1,0:T(1,128)S(1)}, f32[1,4096]{1,0:T(1,128)}, u32[]{:S(2)}) %copy-start.5) | copy-done | bytes 16408
  11.3 0.0 copy-start.1
  11.3 0.0 copy-start.3
  11.3 0.0 copy-start.6
  11.3 0.2 own_rows.1
  11.5 2.7 %collective-permute-done.far = bf16[44,4096]{1,0:T(8,128)(2,1)S(1)} collective-permute-done((bf16[44,4096]{1,0:T(8,128)(2,1)}, bf16[44,4096]{1,0:T(8,128)(2,1)S(1)}, u32[]{:S(2)}, u32[]{:S(2)}) %collective-permute-start) | collective-permute-done | bytes 360480 | tf_op jit(solution)/shard_map/ppermute | solution.py:189
  14.2 1.9 %collective-permute-start.2 = (bf16[44,4096]{1,0:T(8,128)(2,1)S(1)}, bf16[44,4096]{1,0:T(8,128)(2,1)S(1)}, u32[]{:S(2)}, u32[]{:S(2)}) collective-permute-start(bf16[44,4096]{1,0:T(8,128)(2,1)S(1)} %collective-permute-done.far), channel_id=1, source_target_pairs={{0,1},{1,0},{2,3},{3,2},{4,5},{5,4},{6,7},{7,6},{8,9},{9,8},{10,11... | collective-permute-start | bytes 1081352 | tf_op jit(solution)/shard_map/ppermute | solution.py:189
  16.1 0.0 collective-permute-done.1.core
  16.2 1.7 %collective-permute-done.2.farcore = bf16[44,4096]{1,0:T(8,128)(2,1)S(1)} collective-permute-done((bf16[44,4096]{1,0:T(8,128)(2,1)S(1)}, bf16[44,4096]{1,0:T(8,128)(2,1)S(1)}, u32[]{:S(2)}, u32[]{:S(2)}) %collective-permute-start.2) | collective-permute-done | bytes 360480 | tf_op jit(solution)/shard_map/ppermute | solution.py:189
  17.8 0.0 copy-done.1
  17.8 0.0 copy-done.3
  17.8 0.0 copy-done.6
  17.8 7.8 %attention_backward.1 = (bf16[1,176,4096]{2,1,0:T(8,128)(2,1)}, bf16[96,4096]{1,0:T(8,128)(2,1)S(1)}, f32[96,4096]{1,0:T(8,128)S(1)}, bf16[4,32,128]{2,1,0:T(8,128)(2,1)S(1)}) custom-call(f32[44,4096]{1,0:T(8,128)S(1)} %get-tuple-element.20.own, f32[44,128]{1,0:T(8,128)S(1)} %get-tuple-element.21.own_rs, bf16[44,4096]{1,0:T(8,128)(2,1)S(1)} %collective-permute-done.1.core, ...), custom_call_target="tpu_custom_call" | custom-call | flops 1268776960 | bytes 16777216 | tf_op jit(solution)/shard_map/attention_backward/pallas_call | solution.py:195
  25.7 1.9 %collective-permute-start.3 = (bf16[96,4096]{1,0:T(8,128)(2,1)S(1)}, bf16[96,4096]{1,0:T(8,128)(2,1)S(1)}, u32[]{:S(2)}, u32[]{:S(2)}) collective-permute-start(bf16[96,4096]{1,0:T(8,128)(2,1)S(1)} %get-tuple-element.24), channel_id=1, source_target_pairs={{0,1},{1,0},{2,3},{3,2},{4,5},{5,4},{6,7},{7,6},{8,9},{9,8},{10,11... | collective-permute-start | bytes 2359304 | tf_op jit(solution)/shard_map/ppermute | solution.py:189
  27.6 17.4 %all_to_all.10.first = bf16[4,32,128]{2,1,0:T(8,128)(2,1)S(1)} all-to-all(bf16[4,32,128]{2,1,0:T(8,128)(2,1)S(1)} %get-tuple-element.25), channel_id=1, replica_groups=mesh['y'=8,'zh'=4,'x'=4,'zl'=2,'core'=2] {'zh'}, dimensions={0} | all-to-all | bytes 65536 | tf_op jit(solution)/shard_map/all_to_all | solution.py:248
  45.0 0.0 collective-permute-done.3.got
  45.0 0.1 add_core.1
  45.1 3.3 %collective-permute-start.4 = (bf16[64,4096]{1,0:T(8,128)(2,1)S(1)}, bf16[64,4096]{1,0:T(8,128)(2,1)S(1)}, u32[]{:S(2)}, u32[]{:S(2)}) collective-permute-start(bf16[64,4096]{1,0:T(8,128)(2,1)S(1)} %get-tuple-element.30), channel_id=1, source_target_pairs={{0,2},{1,3},{2,0},{3,1},{4,6},{5,7},{6,4},{7,5},{8,10},{9,11},{10,... | collective-permute-start | bytes 1572872 | tf_op jit(solution)/shard_map/ppermute | solution.py:189
  48.5 21.0 %all_to_all.11.second = bf16[32,32,128]{2,1,0:T(8,128)(2,1)S(1)} all-to-all(bf16[32,32,128]{2,1,0:T(8,128)(2,1)S(1)} %sum_near.1), channel_id=1, replica_groups=mesh['y'=8,'zh'=4,'x'=4,'zl'=2,'core'=2] {'y','x'}, dimensions={0} | all-to-all | bytes 524288 | tf_op jit(solution)/shard_map/all_to_all | solution.py:262
  69.5 0.0 collective-permute-done.4.last
  69.5 0.9 %add_far.1 = (bf16[44,4096]{1,0:T(8,128)(2,1)}, f32[1,4096]{1,0:T(1,128)}) custom-call(f32[48,4096]{1,0:T(8,128)S(1)} %get-tuple-element.27.mine, bf16[64,4096]{1,0:T(8,128)(2,1)S(1)} %collective-permute-done.4.last, bf16[32,32,128]{2,1,0:T(8,128)(2,1)S(1)} %all_to_all.11.second), custom_call_target="tpu_custom_call" | custom-call | tf_op jit(solution)/shard_map/add_far/pallas_call | solution.py:195
  (1 shorter events, 0.0 us)
Async XLA Ops:
  0.6 13.6 %collective-permute-start = (bf16[44,4096]{1,0:T(8,128)(2,1)}, bf16[44,4096]{1,0:T(8,128)(2,1)S(1)}, u32[]{:S(2)}, u32[]{:S(2)}) collective-permute-start(bf16[44,4096]{1,0:T(8,128)(2,1)} %own.1), channel_id=1, source_target_pairs={{0,2},{1,3},{2,0},{3,1},{4,6},{5,7},{6,4},{7,5},{8,10},{9,11},{10,... | collective-permute-start | bytes 1081352 | tf_op jit(solution)/shard_map/ppermute | solution.py:189
  4.9 11.2 %collective-permute-start.1 = (bf16[44,4096]{1,0:T(8,128)(2,1)}, bf16[44,4096]{1,0:T(8,128)(2,1)S(1)}, u32[]{:S(2)}, u32[]{:S(2)}) collective-permute-start(bf16[44,4096]{1,0:T(8,128)(2,1)} %own.1), channel_id=1, source_target_pairs={{0,1},{1,0},{2,3},{3,2},{4,5},{5,4},{6,7},{7,6},{8,9},{9,8},{10,11... | collective-permute-start | bytes 1081352 | tf_op jit(solution)/shard_map/ppermute | solution.py:189
  6.8 1.4 %copy-start = (bf16[1,176,4096]{2,1,0:T(8,128)(2,1)S(1)}, bf16[1,176,4096]{2,1,0:T(8,128)(2,1)}, u32[]{:S(2)}) copy-start(bf16[1,176,4096]{2,1,0:T(8,128)(2,1)} %keys.3) | copy-start | bytes 4325380
  8.2 1.4 %copy-start.2 = (bf16[1,176,4096]{2,1,0:T(8,128)(2,1)S(1)}, bf16[1,176,4096]{2,1,0:T(8,128)(2,1)}, u32[]{:S(2)}) copy-start(bf16[1,176,4096]{2,1,0:T(8,128)(2,1)} %cot.3) | copy-start | bytes 4325380
  9.6 1.0 %copy-start.4 = (bf16[44,4096]{1,0:T(8,128)(2,1)S(1)}, bf16[44,4096]{1,0:T(8,128)(2,1)}, u32[]{:S(2)}) copy-start(bf16[44,4096]{1,0:T(8,128)(2,1)} %own.1) | copy-start | bytes 1081348
  10.6 0.7 %copy-start.5 = (f32[1,4096]{1,0:T(1,128)S(1)}, f32[1,4096]{1,0:T(1,128)}, u32[]{:S(2)}) copy-start(f32[1,4096]{1,0:T(1,128)} %gain_ref.1) | copy-start | bytes 49156
  11.3 6.5 %copy-start.1 = (bf16[1,176,4096]{2,1,0:T(8,128)(2,1)S(1)}, bf16[1,176,4096]{2,1,0:T(8,128)(2,1)}, u32[]{:S(2)}) copy-start(bf16[1,176,4096]{2,1,0:T(8,128)(2,1)} %keys.3) | copy-start | bytes 4325380
  11.3 6.5 %copy-start.3 = (bf16[1,176,4096]{2,1,0:T(8,128)(2,1)S(1)}, bf16[1,176,4096]{2,1,0:T(8,128)(2,1)}, u32[]{:S(2)}) copy-start(bf16[1,176,4096]{2,1,0:T(8,128)(2,1)} %cot.3) | copy-start | bytes 4325380
  11.3 6.5 %copy-start.6 = (f32[1,4096]{1,0:T(1,128)S(1)}, f32[1,4096]{1,0:T(1,128)}, u32[]{:S(2)}) copy-start(f32[1,4096]{1,0:T(1,128)} %gain_ref.1) | copy-start | bytes 49156
  14.2 3.6 %collective-permute-start.2 = (bf16[44,4096]{1,0:T(8,128)(2,1)S(1)}, bf16[44,4096]{1,0:T(8,128)(2,1)S(1)}, u32[]{:S(2)}, u32[]{:S(2)}) collective-permute-start(bf16[44,4096]{1,0:T(8,128)(2,1)S(1)} %collective-permute-done.far), channel_id=1, source_target_pairs={{0,1},{1,0},{2,3},{3,2},{4,5},{5,4},{6,7},{7,6},{8,9},{9,8},{10,11... | collective-permute-start | bytes 1081352 | tf_op jit(solution)/shard_map/ppermute | solution.py:189
  25.7 19.3 %collective-permute-start.3 = (bf16[96,4096]{1,0:T(8,128)(2,1)S(1)}, bf16[96,4096]{1,0:T(8,128)(2,1)S(1)}, u32[]{:S(2)}, u32[]{:S(2)}) collective-permute-start(bf16[96,4096]{1,0:T(8,128)(2,1)S(1)} %get-tuple-element.24), channel_id=1, source_target_pairs={{0,1},{1,0},{2,3},{3,2},{4,5},{5,4},{6,7},{7,6},{8,9},{9,8},{10,11... | collective-permute-start | bytes 2359304 | tf_op jit(solution)/shard_map/ppermute | solution.py:189
  45.1 24.4 %collective-permute-start.4 = (bf16[64,4096]{1,0:T(8,128)(2,1)S(1)}, bf16[64,4096]{1,0:T(8,128)(2,1)S(1)}, u32[]{:S(2)}, u32[]{:S(2)}) collective-permute-start(bf16[64,4096]{1,0:T(8,128)(2,1)S(1)} %get-tuple-element.30), channel_id=1, source_target_pairs={{0,2},{1,3},{2,0},{3,1},{4,6},{5,7},{6,4},{7,5},{8,10},{9,11},{10,... | collective-permute-start | bytes 1572872 | tf_op jit(solution)/shard_map/ppermute | solution.py:189

commit v4 on v3

--- a/solution.py
+++ b/solution.py
@@ -11,7 +11,7 @@
 
 NH = 32
 HEAD_DIM = 128
-GROUP = 16
+GROUP = 32
 SLAB = 48
 BF = jnp.bfloat16
 F32 = jnp.float32
@@ -58,16 +58,19 @@
     rs_ref[...] = jnp.broadcast_to(lax.rsqrt(mean + 1e-05), (part, HEAD_DIM))
 
 
-def attention_kernel(peers, own, own_rs, core, far, farcore, keys, cot, gain_ref, gk_ref, give_ref, keep_ref, gterm_ref,
-                     xf, w, rs, macc, gsum, bias0, bias1, gk, gsems):
+def near_kernel(own, core, x_ref, rs_ref):
+    here = pl.multiple_of(2 * own.shape[0] * lax.axis_index("zl"), 8)
+    pair_rows(lax.axis_index("core"), own, core, x_ref, rs_ref, here)
+
+
+def attention_kernel(peers, near, near_rs, far, farcore, keys, cot, gain_ref, gk_ref, give_ref, keep_ref, gterm_ref, xf, rs,
+                     w, macc, gsum, bias0, bias1, gk, gsems):
     part = far.shape[0]
     length, width = xf.shape
     zl = lax.axis_index("zl")
     c = lax.axis_index("core")
-    here = pl.multiple_of(2 * part * zl, 8)
     there = pl.multiple_of(2 * part * (1 - zl), 8)
     pair_rows(c, far, farcore, xf, rs, there)
-    pair_rows(c, own, core, xf, rs, here)
     macc[...] = jnp.zeros_like(macc)
     scale = F32(HEAD_DIM ** (-0.5))
     scale2 = F32(HEAD_DIM ** (-0.5) * math.log2(math.e))
@@ -174,22 +177,23 @@
     here = pl.ds(pl.multiple_of(SLAB * zl, SLAB), SLAB)
     there = pl.ds(pl.multiple_of(SLAB * (1 - zl), SLAB), SLAB)
     mine_ref[...] = keep[here, :] + got[here, :].astype(F32)
-    send_ref[:SLAB] = (keep[there, :] + got[there, :].astype(F32)).astype(send_ref.dtype)
+    rows = send_ref.shape[0]
+    send_ref[...] = (keep[there, :] + got[there, :].astype(F32))[:rows].astype(BF)
 
 
 def final_kernel(mine, last, second, trunk_ref, gains_ref):
     total = jnp.sum(second[...].astype(F32), axis=0)
     for r in range(total.shape[0]):
         gains_ref[0:1, r * HEAD_DIM : (r + 1) * HEAD_DIM] = total[r : r + 1, :]
-    both = mine[...] + last[:SLAB].astype(F32)
-    trunk_ref[...] = both[: trunk_ref.shape[0]].astype(BF)
+    rows = trunk_ref.shape[0]
+    trunk_ref[...] = (mine[...][:rows] + last[...].astype(F32)).astype(BF)
 
 
 def swap(v, bit):
     return lax.ppermute(v, HEAD, [(i, i ^ bit) for i in range(4)])
 
 
-def call(kernel, outs, args, name, hbm_in=(), hbm_out=(), scratch=(), cost=(0, 0), limit=LIMIT):
+def call(kernel, outs, args, name, hbm_in=(), hbm_out=(), scratch=(), cost=(0, 0), limit=LIMIT, alias=None):
     vmem = pl.BlockSpec(memory_space=pltpu.VMEM)
     hbm = pl.BlockSpec(memory_space=pltpu.HBM)
     return pl.pallas_call(
@@ -198,6 +202,7 @@
         in_specs=[hbm if i in hbm_in else vmem for i in range(len(args))],
         out_specs=tuple(hbm if i in hbm_out else vmem for i in range(len(outs))),
         scratch_shapes=list(scratch),
+        input_output_aliases=alias or {},
         compiler_params=pltpu.CompilerParams(vmem_limit_bytes=limit),
         cost_estimate=pl.CostEstimate(flops=cost[0], bytes_accessed=cost[1], transcendentals=0),
         name=name,
@@ -220,21 +225,28 @@
     )
     far, x_own = lax.optimization_barrier((far, x_own))
     farcore = swap(far, 1)
-    grad_keys, give, keep, gterm = call(
+    x_near, rs_near = call(
+        near_kernel,
+        (shape((length, width), F32), shape((length, HEAD_DIM), F32)),
+        (x_own, core),
+        "near_rows",
+    )
+    grad_keys, give, keep, gterm, _, _ = call(
         functools.partial(attention_kernel, near),
         (
             shape((1, length, width), BF),
             shape((2 * SLAB, width), BF),
             shape((2 * SLAB, width), F32),
             shape((near, NH, HEAD_DIM), BF),
+            shape((length, width), F32),
+            shape((length, HEAD_DIM), F32),
         ),
-        (x_own, rs_own, core, far, farcore, keys, grad_out, gains),
+        (x_near, rs_near, far, farcore, keys, grad_out, gains),
         "attention_backward",
         hbm_out=(0,),
+        alias={0: 4, 1: 5},
         scratch=[
             pltpu.VMEM((length, width), F32),
-            pltpu.VMEM((length, width), F32),
-            pltpu.VMEM((length, HEAD_DIM), F32),
             pltpu.VMEM((length, HEAD_DIM), F32),
             pltpu.VMEM((NH, HEAD_DIM), F32),
             pltpu.VMEM((HEAD_DIM, HEAD_DIM), F32),
@@ -245,10 +257,10 @@
         cost=(10 * length * length * width, 16 << 20),
     )
     got = swap(give, 1)
-    first = lax.all_to_all(gterm, "zh", 0, 0, tiled=True)
+    first = lax.all_to_all(gterm, "y", 0, 0, tiled=True)
     got, first = lax.optimization_barrier((got, first))
     mine, send = call(
-        between_kernel, (shape((SLAB, width), F32), shape((64, width), BF)), (keep, got), "add_core"
+        between_kernel, (shape((SLAB, width), F32), shape((part, width), BF)), (keep, got), "add_core"
     )
     send, first = lax.optimization_barrier((send, first))
     last = swap(send, 2)
@@ -259,7 +271,7 @@
         "sum_near",
         cost=(8 << 30, 0),
     )
-    second = lax.all_to_all(wide, ("y", "x"), 0, 0, tiled=True)
+    second = lax.all_to_all(wide, ("zh", "x"), 0, 0, tiled=True)
     grad_trunk, grad_gains = call(
         final_kernel, (shape((part, width), BF), shape((1, width), F32)), (mine, last, second), "add_far"
     )
@@ -274,7 +286,7 @@
     fine = Mesh(mesh.devices.reshape(y, zh, near, 2, 2), ("y", "zh", "x", "zl", "core"))
     dps = ("y", "zh", "x")
     return jax.shard_map(
-        functools.partial(on_device, zh, dp // zh),
+        functools.partial(on_device, y, zh * near),
         mesh=fine,
         in_specs=(
             P(dps + HEAD, None),

time: 70.8 us -> 68.4 us (0.966)
  blocking collectives: 38.4 us -> 36.4 us
  waiting for transfers between devices: 4.39 us -> 3.34 us
    all_to_all x2, blocking collectives: 38.4 us -> 36.4 us  [the longest x1 22.2 us: on_device(): second = lax.all_to_all(wide, ('zh', 'x'), 0, 0, tiled=True)]
    ppermute x5, waiting for transfers between devices: 4.39 us -> 3.34 us  [swap(): return lax.ppermute(v, HEAD, [(i, i ^ bit) for i in range(4)])]
    pallas_call x5 -> x6, Pallas kernels: 9.06 us -> 9.23 us  [call(): pl.pallas_call(kernel, out_shape=outs, in_specs=[hbm if i in hbm_in else...]
  transfers between devices with their start and end apart: 5 -> 5, of which waited for: 2 -> 2; matrix products, arithmetic and copies ran while one was open for 0% -> 0% of each run, Pallas kernels for 0% -> 2%
where the time goes in v4:
time: 68.4 us; the launch traced here: 68 us
  blocking collectives  36.4 us (53%)
  starting transfers between devices  13.8 us (20%)
  Pallas kernels  9.23 us (13%)
  local copies, waits for them, and re-layouts  4.44 us (6%)
  waiting for transfers between devices  3.34 us (5%)
  between operations  0.73 us (1%)
    all_to_all x1, blocking collectives, on_device(): second = lax.all_to_all(wide, ('zh', 'x'), 0, 0, tiled=True)  22.2 us
    all_to_all x1, blocking collectives, on_device(): first = lax.all_to_all(gterm, 'y', 0, 0, tiled=True)  14.3 us
    ppermute x5, starting transfers between devices, swap(): return lax.ppermute(v, HEAD, [(i, i ^ bit) for i in range(4)])  13.8 us
    pallas_call x6, Pallas kernels, call(): pl.pallas_call(kernel, out_shape=outs, in_specs=[hbm if i in hbm_in else...  9.23 us
    unnamed x14, local copies, waits for them, and re-layouts  4.44 us
    ppermute x5, waiting for transfers between devices, swap(): return lax.ppermute(v, HEAD, [(i, i ^ bit) for i in range(4)])  3.34 us
  transfers between devices with their start and end apart: 5, of which 2 were waited for; matrix products, arithmetic and copies ran while one was open for 0% of the time, Pallas kernels for 2%

profile of v4, /device:TPU:8, one launch (start us, length us, event | category | flops | bytes accessed | tf_op | source)
XLA Modules:
  0.0 68.0 jit_solution(8722762867623569053)
XLA Ops:
  0.6 4.3 %collective-permute-start = (bf16[44,4096]{1,0:T(8,128)(2,1)}, bf16[44,4096]{1,0:T(8,128)(2,1)S(1)}, u32[]{:S(2)}, u32[]{:S(2)}) collective-permute-start(bf16[44,4096]{1,0:T(8,128)(2,1)} %own.1), channel_id=1, source_target_pairs={{0,2},{1,3},{2,0},{3,1},{4,6},{5,7},{6,4},{7,5},{8,10},{9,11},{10,... | collective-permute-start | bytes 1081352 | tf_op jit(solution)/shard_map/ppermute | solution.py:193
  4.9 1.9 %collective-permute-start.1 = (bf16[44,4096]{1,0:T(8,128)(2,1)}, bf16[44,4096]{1,0:T(8,128)(2,1)S(1)}, u32[]{:S(2)}, u32[]{:S(2)}) collective-permute-start(bf16[44,4096]{1,0:T(8,128)(2,1)} %own.1), channel_id=1, source_target_pairs={{0,1},{1,0},{2,3},{3,2},{4,5},{5,4},{6,7},{7,6},{8,9},{9,8},{10,11... | collective-permute-start | bytes 1081352 | tf_op jit(solution)/shard_map/ppermute | solution.py:193
  6.8 0.0 copy-start
  6.9 1.4 %copy-done = bf16[1,176,4096]{2,1,0:T(8,128)(2,1)S(1)} copy-done((bf16[1,176,4096]{2,1,0:T(8,128)(2,1)S(1)}, bf16[1,176,4096]{2,1,0:T(8,128)(2,1)}, u32[]{:S(2)}) %copy-start) | copy-done | bytes 1441816
  8.2 0.0 copy-start.2
  8.2 1.4 %copy-done.2 = bf16[1,176,4096]{2,1,0:T(8,128)(2,1)S(1)} copy-done((bf16[1,176,4096]{2,1,0:T(8,128)(2,1)S(1)}, bf16[1,176,4096]{2,1,0:T(8,128)(2,1)}, u32[]{:S(2)}) %copy-start.2) | copy-done | bytes 1441816
  9.6 0.0 copy-start.4
  9.6 1.0 %copy-done.4 = bf16[44,4096]{1,0:T(8,128)(2,1)S(1)} copy-done((bf16[44,4096]{1,0:T(8,128)(2,1)S(1)}, bf16[44,4096]{1,0:T(8,128)(2,1)}, u32[]{:S(2)}) %copy-start.4) | copy-done | bytes 360472
  10.6 0.0 copy-start.5
  10.6 0.7 %copy-done.5 = f32[1,4096]{1,0:T(1,128)S(1)} copy-done((f32[1,4096]{1,0:T(1,128)S(1)}, f32[1,4096]{1,0:T(1,128)}, u32[]{:S(2)}) %copy-start.5) | copy-done | bytes 16408
  11.3 0.0 copy-start.1
  11.3 0.0 copy-start.3
  11.3 0.0 copy-start.6
  11.3 0.8 %own_rows.1 = (f32[44,4096]{1,0:T(8,128)S(1)}, f32[44,128]{1,0:T(8,128)}) custom-call(bf16[44,4096]{1,0:T(8,128)(2,1)S(1)} %copy-done.4, bf16[1,176,4096]{2,1,0:T(8,128)(2,1)S(1)} %copy-done, bf16[1,176,4096]{2,1,0:T(8,128)(2,1)S(1)} %copy-done.2, f32[1,4096]{1,0:T(1,128)S(1)} %copy-done.5), custom_call_target="tpu_custom_call" | custom-call | bytes 8388608 | tf_op jit(solution)/shard_map/own_rows/pallas_call | solution.py:199
  12.1 2.1 %collective-permute-done.far = bf16[44,4096]{1,0:T(8,128)(2,1)S(1)} collective-permute-done((bf16[44,4096]{1,0:T(8,128)(2,1)}, bf16[44,4096]{1,0:T(8,128)(2,1)S(1)}, u32[]{:S(2)}, u32[]{:S(2)}) %collective-permute-start) | collective-permute-done | bytes 360480 | tf_op jit(solution)/shard_map/ppermute | solution.py:193
  14.2 1.9 %collective-permute-start.2 = (bf16[44,4096]{1,0:T(8,128)(2,1)S(1)}, bf16[44,4096]{1,0:T(8,128)(2,1)S(1)}, u32[]{:S(2)}, u32[]{:S(2)}) collective-permute-start(bf16[44,4096]{1,0:T(8,128)(2,1)S(1)} %collective-permute-done.far), channel_id=1, source_target_pairs={{0,1},{1,0},{2,3},{3,2},{4,5},{5,4},{6,7},{7,6},{8,9},{9,8},{10,11... | collective-permute-start | bytes 1081352 | tf_op jit(solution)/shard_map/ppermute | solution.py:193
  16.1 0.0 collective-permute-done.1.core
  16.2 0.4 near_rows.1
  16.6 1.2 %collective-permute-done.2.farcore = bf16[44,4096]{1,0:T(8,128)(2,1)S(1)} collective-permute-done((bf16[44,4096]{1,0:T(8,128)(2,1)S(1)}, bf16[44,4096]{1,0:T(8,128)(2,1)S(1)}, u32[]{:S(2)}, u32[]{:S(2)}) %collective-permute-start.2) | collective-permute-done | bytes 360480 | tf_op jit(solution)/shard_map/ppermute | solution.py:193
  17.8 0.0 copy-done.1
  17.8 0.0 copy-done.3
  17.8 0.0 copy-done.6
  17.8 7.0 %attention_backward.1 = (bf16[1,176,4096]{2,1,0:T(8,128)(2,1)}, bf16[96,4096]{1,0:T(8,128)(2,1)S(1)}, f32[96,4096]{1,0:T(8,128)S(1)}, bf16[8,32,128]{2,1,0:T(8,1...) custom-call(f32[176,4096]{1,0:T(8,128)S(1)} %get-tuple-element.22.nea, ...), custom_call_target="tpu_custom_call", output_to_operand_aliasing={{4}: (0, {}), {5}: (1, {})} | custom-call | flops 1268776960 | bytes 16777216 | tf_op jit(solution)/shard_map/attention_backward/pallas_call | solution.py:199
  24.8 2.0 %collective-permute-start.3 = (bf16[96,4096]{1,0:T(8,128)(2,1)S(1)}, bf16[96,4096]{1,0:T(8,128)(2,1)S(1)}, u32[]{:S(2)}, u32[]{:S(2)}) collective-permute-start(bf16[96,4096]{1,0:T(8,128)(2,1)S(1)} %get-tuple-element.26), channel_id=1, source_target_pairs={{0,1},{1,0},{2,3},{3,2},{4,5},{5,4},{6,7},{7,6},{8,9},{9,8},{10,11... | collective-permute-start | bytes 2359304 | tf_op jit(solution)/shard_map/ppermute | solution.py:193
  26.9 14.3 %all_to_all.10.first = bf16[8,32,128]{2,1,0:T(8,128)(2,1)S(1)} all-to-all(bf16[8,32,128]{2,1,0:T(8,128)(2,1)S(1)} %get-tuple-element.27), channel_id=1, replica_groups=mesh['y'=8,'zh'=4,'x'=4,'zl'=2,'core'=2] {'y'}, dimensions={0} | all-to-all | bytes 131072 | tf_op jit(solution)/shard_map/all_to_all | solution.py:260
  41.1 0.0 collective-permute-done.3.got
  41.1 0.1 add_core.1
  41.3 3.6 %collective-permute-start.4 = (bf16[44,4096]{1,0:T(8,128)(2,1)S(1)}, bf16[44,4096]{1,0:T(8,128)(2,1)S(1)}, u32[]{:S(2)}, u32[]{:S(2)}) collective-permute-start(bf16[44,4096]{1,0:T(8,128)(2,1)S(1)} %get-tuple-element.32), channel_id=1, source_target_pairs={{0,2},{1,3},{2,0},{3,1},{4,6},{5,7},{6,4},{7,5},{8,10},{9,11},{10,... | collective-permute-start | bytes 1081352 | tf_op jit(solution)/shard_map/ppermute | solution.py:193
  45.0 22.2 %all_to_all.11.second = bf16[16,32,128]{2,1,0:T(8,128)(2,1)S(1)} all-to-all(bf16[16,32,128]{2,1,0:T(8,128)(2,1)S(1)} %sum_near.1), channel_id=1, replica_groups=mesh['y'=8,'zh'=4,'x'=4,'zl'=2,'core'=2] {'zh','x'}, dimensions={0} | all-to-all | bytes 262144 | tf_op jit(solution)/shard_map/all_to_all | solution.py:274
  67.1 0.0 collective-permute-done.4.last
  67.1 0.8 %add_far.1 = (bf16[44,4096]{1,0:T(8,128)(2,1)}, f32[1,4096]{1,0:T(1,128)}) custom-call(f32[48,4096]{1,0:T(8,128)S(1)} %get-tuple-element.29.mine, bf16[44,4096]{1,0:T(8,128)(2,1)S(1)} %collective-permute-done.4.last, bf16[16,32,128]{2,1,0:T(8,128)(2,1)S(1)} %all_to_all.11.second), custom_call_target="tpu_custom_call" | custom-call | tf_op jit(solution)/shard_map/add_far/pallas_call | solution.py:199
  (1 shorter events, 0.0 us)
Async XLA Ops:
  0.6 13.6 %collective-permute-start = (bf16[44,4096]{1,0:T(8,128)(2,1)}, bf16[44,4096]{1,0:T(8,128)(2,1)S(1)}, u32[]{:S(2)}, u32[]{:S(2)}) collective-permute-start(bf16[44,4096]{1,0:T(8,128)(2,1)} %own.1), channel_id=1, source_target_pairs={{0,2},{1,3},{2,0},{3,1},{4,6},{5,7},{6,4},{7,5},{8,10},{9,11},{10,... | collective-permute-start | bytes 1081352 | tf_op jit(solution)/shard_map/ppermute | solution.py:193
  4.9 11.2 %collective-permute-start.1 = (bf16[44,4096]{1,0:T(8,128)(2,1)}, bf16[44,4096]{1,0:T(8,128)(2,1)S(1)}, u32[]{:S(2)}, u32[]{:S(2)}) collective-permute-start(bf16[44,4096]{1,0:T(8,128)(2,1)} %own.1), channel_id=1, source_target_pairs={{0,1},{1,0},{2,3},{3,2},{4,5},{5,4},{6,7},{7,6},{8,9},{9,8},{10,11... | collective-permute-start | bytes 1081352 | tf_op jit(solution)/shard_map/ppermute | solution.py:193
  6.8 1.4 %copy-start = (bf16[1,176,4096]{2,1,0:T(8,128)(2,1)S(1)}, bf16[1,176,4096]{2,1,0:T(8,128)(2,1)}, u32[]{:S(2)}) copy-start(bf16[1,176,4096]{2,1,0:T(8,128)(2,1)} %keys.3) | copy-start | bytes 4325380
  8.2 1.4 %copy-start.2 = (bf16[1,176,4096]{2,1,0:T(8,128)(2,1)S(1)}, bf16[1,176,4096]{2,1,0:T(8,128)(2,1)}, u32[]{:S(2)}) copy-start(bf16[1,176,4096]{2,1,0:T(8,128)(2,1)} %cot.3) | copy-start | bytes 4325380
  9.6 1.0 %copy-start.4 = (bf16[44,4096]{1,0:T(8,128)(2,1)S(1)}, bf16[44,4096]{1,0:T(8,128)(2,1)}, u32[]{:S(2)}) copy-start(bf16[44,4096]{1,0:T(8,128)(2,1)} %own.1) | copy-start | bytes 1081348
  10.6 0.7 %copy-start.5 = (f32[1,4096]{1,0:T(1,128)S(1)}, f32[1,4096]{1,0:T(1,128)}, u32[]{:S(2)}) copy-start(f32[1,4096]{1,0:T(1,128)} %gain_ref.1) | copy-start | bytes 49156
  11.3 6.5 %copy-start.1 = (bf16[1,176,4096]{2,1,0:T(8,128)(2,1)S(1)}, bf16[1,176,4096]{2,1,0:T(8,128)(2,1)}, u32[]{:S(2)}) copy-start(bf16[1,176,4096]{2,1,0:T(8,128)(2,1)} %keys.3) | copy-start | bytes 4325380
  11.3 6.5 %copy-start.3 = (bf16[1,176,4096]{2,1,0:T(8,128)(2,1)S(1)}, bf16[1,176,4096]{2,1,0:T(8,128)(2,1)}, u32[]{:S(2)}) copy-start(bf16[1,176,4096]{2,1,0:T(8,128)(2,1)} %cot.3) | copy-start | bytes 4325380
  11.3 6.5 %copy-start.6 = (f32[1,4096]{1,0:T(1,128)S(1)}, f32[1,4096]{1,0:T(1,128)}, u32[]{:S(2)}) copy-start(f32[1,4096]{1,0:T(1,128)} %gain_ref.1) | copy-start | bytes 49156
  14.2 3.6 %collective-permute-start.2 = (bf16[44,4096]{1,0:T(8,128)(2,1)S(1)}, bf16[44,4096]{1,0:T(8,128)(2,1)S(1)}, u32[]{:S(2)}, u32[]{:S(2)}) collective-permute-start(bf16[44,4096]{1,0:T(8,128)(2,1)S(1)} %collective-permute-done.far), channel_id=1, source_target_pairs={{0,1},{1,0},{2,3},{3,2},{4,5},{5,4},{6,7},{7,6},{8,9},{9,8},{10,11... | collective-permute-start | bytes 1081352 | tf_op jit(solution)/shard_map/ppermute | solution.py:193
  24.8 16.3 %collective-permute-start.3 = (bf16[96,4096]{1,0:T(8,128)(2,1)S(1)}, bf16[96,4096]{1,0:T(8,128)(2,1)S(1)}, u32[]{:S(2)}, u32[]{:S(2)}) collective-permute-start(bf16[96,4096]{1,0:T(8,128)(2,1)S(1)} %get-tuple-element.26), channel_id=1, source_target_pairs={{0,1},{1,0},{2,3},{3,2},{4,5},{5,4},{6,7},{7,6},{8,9},{9,8},{10,11... | collective-permute-start | bytes 2359304 | tf_op jit(solution)/shard_map/ppermute | solution.py:193
  41.3 25.8 %collective-permute-start.4 = (bf16[44,4096]{1,0:T(8,128)(2,1)S(1)}, bf16[44,4096]{1,0:T(8,128)(2,1)S(1)}, u32[]{:S(2)}, u32[]{:S(2)}) collective-permute-start(bf16[44,4096]{1,0:T(8,128)(2,1)S(1)} %get-tuple-element.32), channel_id=1, source_target_pairs={{0,2},{1,3},{2,0},{3,1},{4,6},{5,7},{6,4},{7,5},{8,10},{9,11},{10,... | collective-permute-start | bytes 1081352 | tf_op jit(solution)/shard_map/ppermute | solution.py:193

commit v5 on v4

--- a/solution.py
+++ b/solution.py
@@ -11,7 +11,7 @@
 
 NH = 32
 HEAD_DIM = 128
-GROUP = 32
+SENT = 8
 SLAB = 48
 BF = jnp.bfloat16
 F32 = jnp.float32
@@ -22,6 +22,8 @@
 
 
 def columns(a):
+    if isinstance(a, int):
+        return pl.ds(a * HEAD_DIM, HEAD_DIM)
     return pl.ds(pl.multiple_of(a * HEAD_DIM, HEAD_DIM), HEAD_DIM)
 
 
@@ -58,19 +60,38 @@
     rs_ref[...] = jnp.broadcast_to(lax.rsqrt(mean + 1e-05), (part, HEAD_DIM))
 
 
-def near_kernel(own, core, x_ref, rs_ref):
-    here = pl.multiple_of(2 * own.shape[0] * lax.axis_index("zl"), 8)
-    pair_rows(lax.axis_index("core"), own, core, x_ref, rs_ref, here)
-
-
-def attention_kernel(peers, near, near_rs, far, farcore, keys, cot, gain_ref, gk_ref, give_ref, keep_ref, gterm_ref, xf, rs,
+def far_rows(zl, c, ref, x_ref, rs_ref, same):
+    part, width = ref.shape
+    for p in range(4):
+
+        @pl.when((zl == 1 - p // 2) & (c == (p % 2 if same else 1 - p % 2)))
+        def _(p=p):
+            def put(a, acc):
+                sl = columns(a)
+                v = ref[:, sl].astype(F32)
+                x_ref[part * p : part * (p + 1), sl] = v
+                return acc + v * v
+
+            total = lax.fori_loop(0, width // HEAD_DIM, put, jnp.zeros((part, HEAD_DIM), F32), unroll=4)
+            mean = jnp.sum(total, axis=-1, keepdims=True) * (1.0 / width)
+            rs_ref[part * p : part * (p + 1), :] = jnp.broadcast_to(lax.rsqrt(mean + 1e-05), (part, HEAD_DIM))
+
+
+def near_kernel(own, core, far, x_ref, rs_ref):
+    zl = lax.axis_index("zl")
+    c = lax.axis_index("core")
+    here = pl.multiple_of(2 * own.shape[0] * zl, 8)
+    pair_rows(c, own, core, x_ref, rs_ref, here)
+    far_rows(zl, c, far, x_ref, rs_ref, True)
+
+
+def attention_kernel(peers, near, near_rs, farcore, keys, cot, gain_ref, gk_ref, give_ref, keep_ref, gterm_ref, xf, rs,
                      w, macc, gsum, bias0, bias1, gk, gsems):
-    part = far.shape[0]
+    part = farcore.shape[0]
     length, width = xf.shape
     zl = lax.axis_index("zl")
     c = lax.axis_index("core")
-    there = pl.multiple_of(2 * part * (1 - zl), 8)
-    pair_rows(c, far, farcore, xf, rs, there)
+    far_rows(zl, c, farcore, xf, rs, False)
     macc[...] = jnp.zeros_like(macc)
     scale = F32(HEAD_DIM ** (-0.5))
     scale2 = F32(HEAD_DIM ** (-0.5) * math.log2(math.e))
@@ -123,24 +144,23 @@
         return nd * gain
 
     def send_group(i):
-        sl = pl.ds(pl.multiple_of(i * GROUP * HEAD_DIM, GROUP * HEAD_DIM), GROUP * HEAD_DIM)
+        sl = pl.ds(i * SENT * HEAD_DIM, SENT * HEAD_DIM)
         return pltpu.make_async_copy(gk.at[0, :, sl], gk_ref.at[0, :, sl], gsems.at[i])
 
-    def heads(i, _):
-        first, second, mean = {}, {}, None
-        for step in range(GROUP + 2):
-            if step < GROUP:
-                first[step] = begin(i * GROUP + step)
-            if 0 <= step - 1 < GROUP:
-                second[step - 1] = middle(*first.pop(step - 1))
-            if 0 <= step - 2 < GROUP:
-                one = end(i * GROUP + step - 2, *second.pop(step - 2))
-                mean = one if mean is None else mean + one
-        macc[...] += mean
-        send_group(i).start()
-        return 0
-
-    lax.fori_loop(0, NH // GROUP, heads, 0)
+    first, second, mean = {}, {}, None
+    for step in range(NH + 2):
+        if step < NH:
+            first[step] = begin(step)
+        if 0 <= step - 1 < NH:
+            second[step - 1] = middle(*first.pop(step - 1))
+        if 0 <= step - 2 < NH:
+            one = end(step - 2, *second.pop(step - 2))
+            mean = one if mean is None else mean + one
+            if (step - 1) % SENT == 0:
+                send_group((step - 1) // SENT - 1).start()
+            if (step - 1) % 8 == 0:
+                macc[...] += mean
+                mean = None
     for i in range(peers):
         gterm_ref[i] = gsum[...].astype(BF)
     r = rs[...]
@@ -162,7 +182,7 @@
 
             lax.fori_loop(0, width // HEAD_DIM, finish, 0, unroll=2)
 
-    for i in range(NH // GROUP):
+    for i in range(NH // SENT):
         send_group(i).wait()
 
 
@@ -228,7 +248,7 @@
     x_near, rs_near = call(
         near_kernel,
         (shape((length, width), F32), shape((length, HEAD_DIM), F32)),
-        (x_own, core),
+        (x_own, core, far),
         "near_rows",
     )
     grad_keys, give, keep, gterm, _, _ = call(
@@ -241,7 +261,7 @@
             shape((length, width), F32),
             shape((length, HEAD_DIM), F32),
         ),
-        (x_near, rs_near, far, farcore, keys, grad_out, gains),
+        (x_near, rs_near, farcore, keys, grad_out, gains),
         "attention_backward",
         hbm_out=(0,),
         alias={0: 4, 1: 5},
@@ -252,7 +272,7 @@
             pltpu.VMEM((HEAD_DIM, HEAD_DIM), F32),
             pltpu.VMEM((length - HEAD_DIM, length - HEAD_DIM), F32),
             pltpu.VMEM((1, length, width), BF),
-            pltpu.SemaphoreType.DMA((NH // GROUP,)),
+            pltpu.SemaphoreType.DMA((NH // SENT,)),
         ],
         cost=(10 * length * length * width, 16 << 20),
     )

time: 68.4 us -> 68.2 us (level)
  no operation moved by 1% of the time
where the time goes in v5:
time: 68.2 us; the launch traced here: 67.8 us
  blocking collectives  36.4 us (53%)
  starting transfers between devices  13.7 us (20%)
  Pallas kernels  9.38 us (14%)
  local copies, waits for them, and re-layouts  4.44 us (7%)
  waiting for transfers between devices  3.09 us (5%)
  between operations  0.73 us (1%)
    all_to_all x1, blocking collectives, on_device(): second = lax.all_to_all(wide, ('zh', 'x'), 0, 0, tiled=True)  22.2 us
    all_to_all x1, blocking collectives, on_device(): first = lax.all_to_all(gterm, 'y', 0, 0, tiled=True)  14.3 us
    ppermute x5, starting transfers between devices, swap(): return lax.ppermute(v, HEAD, [(i, i ^ bit) for i in range(4)])  13.7 us
    pallas_call x6, Pallas kernels, call(): pl.pallas_call(kernel, out_shape=outs, in_specs=[hbm if i in hbm_in else...  9.38 us
    unnamed x14, local copies, waits for them, and re-layouts  4.44 us
    ppermute x5, waiting for transfers between devices, swap(): return lax.ppermute(v, HEAD, [(i, i ^ bit) for i in range(4)])  3.09 us
  transfers between devices with their start and end apart: 5, of which 2 were waited for; matrix products, arithmetic and copies ran while one was open for 0% of the time, Pallas kernels for 2%

profile of v5, /device:TPU:8, one launch (start us, length us, event | category | flops | bytes accessed | tf_op | source)
XLA Modules:
  0.0 67.8 jit_solution(17217066916427433545)
XLA Ops:
  0.6 4.3 %collective-permute-start = (bf16[44,4096]{1,0:T(8,128)(2,1)}, bf16[44,4096]{1,0:T(8,128)(2,1)S(1)}, u32[]{:S(2)}, u32[]{:S(2)}) collective-permute-start(bf16[44,4096]{1,0:T(8,128)(2,1)} %own.1), channel_id=1, source_target_pairs={{0,2},{1,3},{2,0},{3,1},{4,6},{5,7},{6,4},{7,5},{8,10},{9,11},{10,... | collective-permute-start | bytes 1081352 | tf_op jit(solution)/shard_map/ppermute | solution.py:213
  4.9 1.9 %collective-permute-start.1 = (bf16[44,4096]{1,0:T(8,128)(2,1)}, bf16[44,4096]{1,0:T(8,128)(2,1)S(1)}, u32[]{:S(2)}, u32[]{:S(2)}) collective-permute-start(bf16[44,4096]{1,0:T(8,128)(2,1)} %own.1), channel_id=1, source_target_pairs={{0,1},{1,0},{2,3},{3,2},{4,5},{5,4},{6,7},{7,6},{8,9},{9,8},{10,11... | collective-permute-start | bytes 1081352 | tf_op jit(solution)/shard_map/ppermute | solution.py:213
  6.8 0.0 copy-start
  6.9 1.4 %copy-done = bf16[1,176,4096]{2,1,0:T(8,128)(2,1)S(1)} copy-done((bf16[1,176,4096]{2,1,0:T(8,128)(2,1)S(1)}, bf16[1,176,4096]{2,1,0:T(8,128)(2,1)}, u32[]{:S(2)}) %copy-start) | copy-done | bytes 1441816
  8.2 0.0 copy-start.2
  8.2 1.4 %copy-done.2 = bf16[1,176,4096]{2,1,0:T(8,128)(2,1)S(1)} copy-done((bf16[1,176,4096]{2,1,0:T(8,128)(2,1)S(1)}, bf16[1,176,4096]{2,1,0:T(8,128)(2,1)}, u32[]{:S(2)}) %copy-start.2) | copy-done | bytes 1441816
  9.6 0.0 copy-start.4
  9.6 1.0 %copy-done.4 = bf16[44,4096]{1,0:T(8,128)(2,1)S(1)} copy-done((bf16[44,4096]{1,0:T(8,128)(2,1)S(1)}, bf16[44,4096]{1,0:T(8,128)(2,1)}, u32[]{:S(2)}) %copy-start.4) | copy-done | bytes 360472
  10.6 0.0 copy-start.5
  10.6 0.7 %copy-done.5 = f32[1,4096]{1,0:T(1,128)S(1)} copy-done((f32[1,4096]{1,0:T(1,128)S(1)}, f32[1,4096]{1,0:T(1,128)}, u32[]{:S(2)}) %copy-start.5) | copy-done | bytes 16408
  11.3 0.0 copy-start.3
  11.3 0.8 %own_rows.1 = (f32[44,4096]{1,0:T(8,128)S(1)}, f32[44,128]{1,0:T(8,128)}) custom-call(bf16[44,4096]{1,0:T(8,128)(2,1)S(1)} %copy-done.4, bf16[1,176,4096]{2,1,0:T(8,128)(2,1)S(1)} %copy-done, bf16[1,176,4096]{2,1,0:T(8,128)(2,1)S(1)} %copy-done.2, f32[1,4096]{1,0:T(1,128)S(1)} %copy-done.5), custom_call_target="tpu_custom_call" | custom-call | bytes 8388608 | tf_op jit(solution)/shard_map/own_rows/pallas_call | solution.py:219
  12.1 0.0 copy-start.1
  12.1 0.0 copy-start.6
  12.1 2.1 %collective-permute-done.far = bf16[44,4096]{1,0:T(8,128)(2,1)S(1)} collective-permute-done((bf16[44,4096]{1,0:T(8,128)(2,1)}, bf16[44,4096]{1,0:T(8,128)(2,1)S(1)}, u32[]{:S(2)}, u32[]{:S(2)}) %collective-permute-start) | collective-permute-done | bytes 360480 | tf_op jit(solution)/shard_map/ppermute | solution.py:213
  14.2 1.9 %collective-permute-start.2 = (bf16[44,4096]{1,0:T(8,128)(2,1)S(1)}, bf16[44,4096]{1,0:T(8,128)(2,1)S(1)}, u32[]{:S(2)}, u32[]{:S(2)}) collective-permute-start(bf16[44,4096]{1,0:T(8,128)(2,1)S(1)} %collective-permute-done.far), channel_id=1, source_target_pairs={{0,1},{1,0},{2,3},{3,2},{4,5},{5,4},{6,7},{7,6},{8,9},{9,8},{10,11... | collective-permute-start | bytes 1081352 | tf_op jit(solution)/shard_map/ppermute | solution.py:213
  16.1 0.0 collective-permute-done.1.core
  16.2 0.7 near_rows.1
  16.8 1.0 %collective-permute-done.2.farcore = bf16[44,4096]{1,0:T(8,128)(2,1)S(1)} collective-permute-done((bf16[44,4096]{1,0:T(8,128)(2,1)S(1)}, bf16[44,4096]{1,0:T(8,128)(2,1)S(1)}, u32[]{:S(2)}, u32[]{:S(2)}) %collective-permute-start.2) | collective-permute-done | bytes 360480 | tf_op jit(solution)/shard_map/ppermute | solution.py:213
  17.8 0.0 copy-done.3
  17.8 0.0 copy-done.1
  17.8 0.0 copy-done.6
  17.8 6.9 %attention_backward.1 = (bf16[1,176,4096]{2,1,0:T(8,128)(2,1)}, bf16[96,4096]{1,0:T(8,128)(2,1)S(1)}, f32[96,4096]{1,0:T(8,128)S(1)}, bf16[8,32,128]{2,1,0:T(8,1...) custom-call(f32[176,4096]{1,0:T(8,128)S(1)} %get-tuple-element.23.nea, ...), custom_call_target="tpu_custom_call", output_to_operand_aliasing={{4}: (0, {}), {5}: (1, {})} | custom-call | flops 1268776960 | bytes 16777216 | tf_op jit(solution)/shard_map/attention_backward/pallas_call | solution.py:219
  24.7 1.9 %collective-permute-start.3 = (bf16[96,4096]{1,0:T(8,128)(2,1)S(1)}, bf16[96,4096]{1,0:T(8,128)(2,1)S(1)}, u32[]{:S(2)}, u32[]{:S(2)}) collective-permute-start(bf16[96,4096]{1,0:T(8,128)(2,1)S(1)} %get-tuple-element.26), channel_id=1, source_target_pairs={{0,1},{1,0},{2,3},{3,2},{4,5},{5,4},{6,7},{7,6},{8,9},{9,8},{10,11... | collective-permute-start | bytes 2359304 | tf_op jit(solution)/shard_map/ppermute | solution.py:213
  26.7 14.3 %all_to_all.10.first = bf16[8,32,128]{2,1,0:T(8,128)(2,1)S(1)} all-to-all(bf16[8,32,128]{2,1,0:T(8,128)(2,1)S(1)} %get-tuple-element.27), channel_id=1, replica_groups=mesh['y'=8,'zh'=4,'x'=4,'zl'=2,'core'=2] {'y'}, dimensions={0} | all-to-all | bytes 131072 | tf_op jit(solution)/shard_map/all_to_all | solution.py:280
  40.9 0.0 collective-permute-done.3.got
  40.9 0.1 add_core.1
  41.1 3.7 %collective-permute-start.4 = (bf16[44,4096]{1,0:T(8,128)(2,1)S(1)}, bf16[44,4096]{1,0:T(8,128)(2,1)S(1)}, u32[]{:S(2)}, u32[]{:S(2)}) collective-permute-start(bf16[44,4096]{1,0:T(8,128)(2,1)S(1)} %get-tuple-element.32), channel_id=1, source_target_pairs={{0,2},{1,3},{2,0},{3,1},{4,6},{5,7},{6,4},{7,5},{8,10},{9,11},{10,... | collective-permute-start | bytes 1081352 | tf_op jit(solution)/shard_map/ppermute | solution.py:213
  44.8 22.2 %all_to_all.11.second = bf16[16,32,128]{2,1,0:T(8,128)(2,1)S(1)} all-to-all(bf16[16,32,128]{2,1,0:T(8,128)(2,1)S(1)} %sum_near.1), channel_id=1, replica_groups=mesh['y'=8,'zh'=4,'x'=4,'zl'=2,'core'=2] {'zh','x'}, dimensions={0} | all-to-all | bytes 262144 | tf_op jit(solution)/shard_map/all_to_all | solution.py:294
  66.9 0.0 collective-permute-done.4.last
  66.9 0.8 %add_far.1 = (bf16[44,4096]{1,0:T(8,128)(2,1)}, f32[1,4096]{1,0:T(1,128)}) custom-call(f32[48,4096]{1,0:T(8,128)S(1)} %get-tuple-element.29.mine, bf16[44,4096]{1,0:T(8,128)(2,1)S(1)} %collective-permute-done.4.last, bf16[16,32,128]{2,1,0:T(8,128)(2,1)S(1)} %all_to_all.11.second), custom_call_target="tpu_custom_call" | custom-call | tf_op jit(solution)/shard_map/add_far/pallas_call | solution.py:219
  (1 shorter events, 0.0 us)
Async XLA Ops:
  0.6 13.6 %collective-permute-start = (bf16[44,4096]{1,0:T(8,128)(2,1)}, bf16[44,4096]{1,0:T(8,128)(2,1)S(1)}, u32[]{:S(2)}, u32[]{:S(2)}) collective-permute-start(bf16[44,4096]{1,0:T(8,128)(2,1)} %own.1), channel_id=1, source_target_pairs={{0,2},{1,3},{2,0},{3,1},{4,6},{5,7},{6,4},{7,5},{8,10},{9,11},{10,... | collective-permute-start | bytes 1081352 | tf_op jit(solution)/shard_map/ppermute | solution.py:213
  4.9 11.2 %collective-permute-start.1 = (bf16[44,4096]{1,0:T(8,128)(2,1)}, bf16[44,4096]{1,0:T(8,128)(2,1)S(1)}, u32[]{:S(2)}, u32[]{:S(2)}) collective-permute-start(bf16[44,4096]{1,0:T(8,128)(2,1)} %own.1), channel_id=1, source_target_pairs={{0,1},{1,0},{2,3},{3,2},{4,5},{5,4},{6,7},{7,6},{8,9},{9,8},{10,11... | collective-permute-start | bytes 1081352 | tf_op jit(solution)/shard_map/ppermute | solution.py:213
  6.8 1.4 %copy-start = (bf16[1,176,4096]{2,1,0:T(8,128)(2,1)S(1)}, bf16[1,176,4096]{2,1,0:T(8,128)(2,1)}, u32[]{:S(2)}) copy-start(bf16[1,176,4096]{2,1,0:T(8,128)(2,1)} %keys.3) | copy-start | bytes 4325380
  8.2 1.4 %copy-start.2 = (bf16[1,176,4096]{2,1,0:T(8,128)(2,1)S(1)}, bf16[1,176,4096]{2,1,0:T(8,128)(2,1)}, u32[]{:S(2)}) copy-start(bf16[1,176,4096]{2,1,0:T(8,128)(2,1)} %cot.3) | copy-start | bytes 4325380
  9.6 1.0 %copy-start.4 = (bf16[44,4096]{1,0:T(8,128)(2,1)S(1)}, bf16[44,4096]{1,0:T(8,128)(2,1)}, u32[]{:S(2)}) copy-start(bf16[44,4096]{1,0:T(8,128)(2,1)} %own.1) | copy-start | bytes 1081348
  10.6 0.7 %copy-start.5 = (f32[1,4096]{1,0:T(1,128)S(1)}, f32[1,4096]{1,0:T(1,128)}, u32[]{:S(2)}) copy-start(f32[1,4096]{1,0:T(1,128)} %gain_ref.1) | copy-start | bytes 49156
  11.3 6.5 %copy-start.3 = (bf16[1,176,4096]{2,1,0:T(8,128)(2,1)S(1)}, bf16[1,176,4096]{2,1,0:T(8,128)(2,1)}, u32[]{:S(2)}) copy-start(bf16[1,176,4096]{2,1,0:T(8,128)(2,1)} %cot.3) | copy-start | bytes 4325380
  12.1 5.7 %copy-start.1 = (bf16[1,176,4096]{2,1,0:T(8,128)(2,1)S(1)}, bf16[1,176,4096]{2,1,0:T(8,128)(2,1)}, u32[]{:S(2)}) copy-start(bf16[1,176,4096]{2,1,0:T(8,128)(2,1)} %keys.3) | copy-start | bytes 4325380
  12.1 5.7 %copy-start.6 = (f32[1,4096]{1,0:T(1,128)S(1)}, f32[1,4096]{1,0:T(1,128)}, u32[]{:S(2)}) copy-start(f32[1,4096]{1,0:T(1,128)} %gain_ref.1) | copy-start | bytes 49156
  14.2 3.6 %collective-permute-start.2 = (bf16[44,4096]{1,0:T(8,128)(2,1)S(1)}, bf16[44,4096]{1,0:T(8,128)(2,1)S(1)}, u32[]{:S(2)}, u32[]{:S(2)}) collective-permute-start(bf16[44,4096]{1,0:T(8,128)(2,1)S(1)} %collective-permute-done.far), channel_id=1, source_target_pairs={{0,1},{1,0},{2,3},{3,2},{4,5},{5,4},{6,7},{7,6},{8,9},{9,8},{10,11... | collective-permute-start | bytes 1081352 | tf_op jit(solution)/shard_map/ppermute | solution.py:213
  24.7 16.2 %collective-permute-start.3 = (bf16[96,4096]{1,0:T(8,128)(2,1)S(1)}, bf16[96,4096]{1,0:T(8,128)(2,1)S(1)}, u32[]{:S(2)}, u32[]{:S(2)}) collective-permute-start(bf16[96,4096]{1,0:T(8,128)(2,1)S(1)} %get-tuple-element.26), channel_id=1, source_target_pairs={{0,1},{1,0},{2,3},{3,2},{4,5},{5,4},{6,7},{7,6},{8,9},{9,8},{10,11... | collective-permute-start | bytes 2359304 | tf_op jit(solution)/shard_map/ppermute | solution.py:213
  41.1 25.9 %collective-permute-start.4 = (bf16[44,4096]{1,0:T(8,128)(2,1)S(1)}, bf16[44,4096]{1,0:T(8,128)(2,1)S(1)}, u32[]{:S(2)}, u32[]{:S(2)}) collective-permute-start(bf16[44,4096]{1,0:T(8,128)(2,1)S(1)} %get-tuple-element.32), channel_id=1, source_target_pairs={{0,2},{1,3},{2,0},{3,1},{4,6},{5,7},{6,4},{7,5},{8,10},{9,11},{10,... | collective-permute-start | bytes 1081352 | tf_op jit(solution)/shard_map/ppermute | solution.py:213

commit v6 on v5

--- a/solution.py
+++ b/solution.py
@@ -277,13 +277,11 @@
         cost=(10 * length * length * width, 16 << 20),
     )
     got = swap(give, 1)
+    mine, send = call(
+        between_kernel, (shape((SLAB, width), F32), shape((part, width), BF)), (keep, got), "add_core", cost=(0, 0)
+    )
+    last = swap(send, 2)
     first = lax.all_to_all(gterm, "y", 0, 0, tiled=True)
-    got, first = lax.optimization_barrier((got, first))
-    mine, send = call(
-        between_kernel, (shape((SLAB, width), F32), shape((part, width), BF)), (keep, got), "add_core"
-    )
-    send, first = lax.optimization_barrier((send, first))
-    last = swap(send, 2)
     (wide,) = call(
         functools.partial(spread_kernel, rest),
         (shape((rest, NH, HEAD_DIM), BF),),

time: 68.2 us -> 65.7 us (0.963)
  blocking collectives: 36.4 us -> 22.5 us
  starting transfers between devices: 13.7 us -> 21.3 us
  waiting for transfers between devices: 3.09 us -> 5.51 us
  Pallas kernels: 9.38 us -> 10.7 us
    all_to_all x1 -> x0, blocking collectives: 14.3 us -> none  [on_device(): first = lax.all_to_all(gterm, 'y', 0, 0, tiled=True)]
    all_to_all x0 -> x1, starting transfers between devices: none -> 7.56 us  [on_device(): first = lax.all_to_all(gterm, 'y', 0, 0, tiled=True)]
    all_to_all x0 -> x1, waiting for transfers between devices: none -> 2.42 us  [on_device(): first = lax.all_to_all(gterm, 'y', 0, 0, tiled=True)]
    pallas_call x6, Pallas kernels: 9.38 us -> 10.7 us  [call(): pl.pallas_call(kernel, out_shape=outs, in_specs=[hbm if i in hbm_in else...]
  transfers between devices with their start and end apart: 5 -> 6, of which waited for: 2 -> 3; matrix products, arithmetic and copies ran while one was open for 0% -> 0% of each run, Pallas kernels for 2% -> 4%
where the time goes in v6:
time: 65.7 us; the launch traced here: 65.2 us
  blocking collectives  22.5 us (34%)
  starting transfers between devices  21.3 us (32%)
  Pallas kernels  10.7 us (16%)
  waiting for transfers between devices  5.51 us (8%)
  local copies, waits for them, and re-layouts  4.44 us (7%)
  between operations  0.72 us (1%)
    all_to_all x1, blocking collectives, on_device(): second = lax.all_to_all(wide, ('zh', 'x'), 0, 0, tiled=True)  22.5 us
    ppermute x5, starting transfers between devices, swap(): return lax.ppermute(v, HEAD, [(i, i ^ bit) for i in range(4)])  13.7 us
    pallas_call x6, Pallas kernels, call(): pl.pallas_call(kernel, out_shape=outs, in_specs=[hbm if i in hbm_in else...  10.7 us
    all_to_all x1, starting transfers between devices, on_device(): first = lax.all_to_all(gterm, 'y', 0, 0, tiled=True)  7.56 us
    unnamed x14, local copies, waits for them, and re-layouts  4.44 us
    ppermute x5, waiting for transfers between devices, swap(): return lax.ppermute(v, HEAD, [(i, i ^ bit) for i in range(4)])  3.09 us
    all_to_all x1, waiting for transfers between devices, on_device(): first = lax.all_to_all(gterm, 'y', 0, 0, tiled=True)  2.42 us
  transfers between devices with their start and end apart: 6, of which 3 were waited for; matrix products, arithmetic and copies ran while one was open for 0% of the time, Pallas kernels for 4%

profile of v6, /device:TPU:8, one launch (start us, length us, event | category | flops | bytes accessed | tf_op | source)
XLA Modules:
  0.0 65.2 jit_solution(14134975389541895675)
XLA Ops:
  0.6 4.3 %collective-permute-start = (bf16[44,4096]{1,0:T(8,128)(2,1)}, bf16[44,4096]{1,0:T(8,128)(2,1)S(1)}, u32[]{:S(2)}, u32[]{:S(2)}) collective-permute-start(bf16[44,4096]{1,0:T(8,128)(2,1)} %own.1), channel_id=1, source_target_pairs={{0,2},{1,3},{2,0},{3,1},{4,6},{5,7},{6,4},{7,5},{8,10},{9,11},{10,... | collective-permute-start | bytes 1081352 | tf_op jit(solution)/shard_map/ppermute | solution.py:213
  4.9 1.9 %collective-permute-start.1 = (bf16[44,4096]{1,0:T(8,128)(2,1)}, bf16[44,4096]{1,0:T(8,128)(2,1)S(1)}, u32[]{:S(2)}, u32[]{:S(2)}) collective-permute-start(bf16[44,4096]{1,0:T(8,128)(2,1)} %own.1), channel_id=1, source_target_pairs={{0,1},{1,0},{2,3},{3,2},{4,5},{5,4},{6,7},{7,6},{8,9},{9,8},{10,11... | collective-permute-start | bytes 1081352 | tf_op jit(solution)/shard_map/ppermute | solution.py:213
  6.8 0.0 copy-start
  6.9 1.4 %copy-done = bf16[1,176,4096]{2,1,0:T(8,128)(2,1)S(1)} copy-done((bf16[1,176,4096]{2,1,0:T(8,128)(2,1)S(1)}, bf16[1,176,4096]{2,1,0:T(8,128)(2,1)}, u32[]{:S(2)}) %copy-start) | copy-done | bytes 1441816
  8.2 0.0 copy-start.2
  8.2 1.4 %copy-done.2 = bf16[1,176,4096]{2,1,0:T(8,128)(2,1)S(1)} copy-done((bf16[1,176,4096]{2,1,0:T(8,128)(2,1)S(1)}, bf16[1,176,4096]{2,1,0:T(8,128)(2,1)}, u32[]{:S(2)}) %copy-start.2) | copy-done | bytes 1441816
  9.6 0.0 copy-start.4
  9.6 1.0 %copy-done.4 = bf16[44,4096]{1,0:T(8,128)(2,1)S(1)} copy-done((bf16[44,4096]{1,0:T(8,128)(2,1)S(1)}, bf16[44,4096]{1,0:T(8,128)(2,1)}, u32[]{:S(2)}) %copy-start.4) | copy-done | bytes 360472
  10.6 0.0 copy-start.5
  10.6 0.7 %copy-done.5 = f32[1,4096]{1,0:T(1,128)S(1)} copy-done((f32[1,4096]{1,0:T(1,128)S(1)}, f32[1,4096]{1,0:T(1,128)}, u32[]{:S(2)}) %copy-start.5) | copy-done | bytes 16408
  11.3 0.0 copy-start.3
  11.3 0.8 %own_rows.1 = (f32[44,4096]{1,0:T(8,128)S(1)}, f32[44,128]{1,0:T(8,128)}) custom-call(bf16[44,4096]{1,0:T(8,128)(2,1)S(1)} %copy-done.4, bf16[1,176,4096]{2,1,0:T(8,128)(2,1)S(1)} %copy-done, bf16[1,176,4096]{2,1,0:T(8,128)(2,1)S(1)} %copy-done.2, f32[1,4096]{1,0:T(1,128)S(1)} %copy-done.5), custom_call_target="tpu_custom_call" | custom-call | bytes 8388608 | tf_op jit(solution)/shard_map/own_rows/pallas_call | solution.py:219
  12.1 0.0 copy-start.1
  12.1 0.0 copy-start.6
  12.1 2.1 %collective-permute-done.far = bf16[44,4096]{1,0:T(8,128)(2,1)S(1)} collective-permute-done((bf16[44,4096]{1,0:T(8,128)(2,1)}, bf16[44,4096]{1,0:T(8,128)(2,1)S(1)}, u32[]{:S(2)}, u32[]{:S(2)}) %collective-permute-start) | collective-permute-done | bytes 360480 | tf_op jit(solution)/shard_map/ppermute | solution.py:213
  14.2 1.9 %collective-permute-start.2 = (bf16[44,4096]{1,0:T(8,128)(2,1)S(1)}, bf16[44,4096]{1,0:T(8,128)(2,1)S(1)}, u32[]{:S(2)}, u32[]{:S(2)}) collective-permute-start(bf16[44,4096]{1,0:T(8,128)(2,1)S(1)} %collective-permute-done.far), channel_id=1, source_target_pairs={{0,1},{1,0},{2,3},{3,2},{4,5},{5,4},{6,7},{7,6},{8,9},{9,8},{10,11... | collective-permute-start | bytes 1081352 | tf_op jit(solution)/shard_map/ppermute | solution.py:213
  16.1 0.0 collective-permute-done.1.core
  16.2 0.7 %near_rows.1 = (f32[176,4096]{1,0:T(8,128)S(1)}, f32[176,128]{1,0:T(8,128)S(1)}) custom-call(f32[44,4096]{1,0:T(8,128)S(1)} %get-tuple-element.17.own, bf16[44,4096]{1,0:T(8,128)(2,1)S(1)} %collective-permute-done.1.core, bf16[44,4096]{1,0:T(8,128)(2,1)S(1)} %collective-permute-done.far), custom_call_target="tpu_custom_call" | custom-call | tf_op jit(solution)/shard_map/near_rows/pallas_call | solution.py:219
  16.8 1.0 %collective-permute-done.2.farcore = bf16[44,4096]{1,0:T(8,128)(2,1)S(1)} collective-permute-done((bf16[44,4096]{1,0:T(8,128)(2,1)S(1)}, bf16[44,4096]{1,0:T(8,128)(2,1)S(1)}, u32[]{:S(2)}, u32[]{:S(2)}) %collective-permute-start.2) | collective-permute-done | bytes 360480 | tf_op jit(solution)/shard_map/ppermute | solution.py:213
  17.8 0.0 copy-done.3
  17.8 0.0 copy-done.1
  17.8 0.0 copy-done.6
  17.8 7.5 %attention_backward.1 = (bf16[1,176,4096]{2,1,0:T(8,128)(2,1)}, bf16[96,4096]{1,0:T(8,128)(2,1)S(1)}, f32[96,4096]{1,0:T(8,128)S(1)}, bf16[8,32,128]{2,1,0:T(8,1...) custom-call(f32[176,4096]{1,0:T(8,128)S(1)} %get-tuple-element.19.near, ...), custom_call_target="tpu_custom_call", output_to_operand_aliasing={{4}: (0, {}), {5}: (1, {})} | custom-call | flops 1268776960 | bytes 16777216 | tf_op jit(solution)/shard_map/attention_backward/pallas_call | solution.py:219
  25.4 2.0 %collective-permute-start.3 = (bf16[96,4096]{1,0:T(8,128)(2,1)S(1)}, bf16[96,4096]{1,0:T(8,128)(2,1)S(1)}, u32[]{:S(2)}, u32[]{:S(2)}) collective-permute-start(bf16[96,4096]{1,0:T(8,128)(2,1)S(1)} %get-tuple-element.22), channel_id=1, source_target_pairs={{0,1},{1,0},{2,3},{3,2},{4,5},{5,4},{6,7},{7,6},{8,9},{9,8},{10,11... | collective-permute-start | bytes 2359304 | tf_op jit(solution)/shard_map/ppermute | solution.py:213
  27.3 7.6 %all-to-all-start = ((bf16[8,32,128]{2,1,0:T(8,128)(2,1)}), bf16[8,32,128]{2,1,0:T(8,128)(2,1)S(1)}, u32[]{:S(2)}, u32[]{:S(2)}) async-start(bf16[8,32,128]{2,1,0:T(8,128)(2,1)} %get-tuple-element.25), calls=%async_computation | async-start | bytes 131072 | tf_op jit(solution)/shard_map/all_to_all | solution.py:284
  34.9 0.0 collective-permute-done.3.got
  34.9 0.9 %add_core.1 = (f32[48,4096]{1,0:T(8,128)S(1)}, bf16[44,4096]{1,0:T(8,128)(2,1)}) custom-call(f32[96,4096]{1,0:T(8,128)S(1)} %get-tuple-element.21.keep, bf16[96,4096]{1,0:T(8,128)(2,1)S(1)} %collective-permute-done.3.got), custom_call_target="tpu_custom_call" | custom-call | tf_op jit(solution)/shard_map/add_core/pallas_call | solution.py:219
  35.7 3.6 %collective-permute-start.4 = (bf16[44,4096]{1,0:T(8,128)(2,1)}, bf16[44,4096]{1,0:T(8,128)(2,1)S(1)}, u32[]{:S(2)}, u32[]{:S(2)}) collective-permute-start(bf16[44,4096]{1,0:T(8,128)(2,1)} %get-tuple-element.24), channel_id=1, source_target_pairs={{0,2},{1,3},{2,0},{3,1},{4,6},{5,7},{6,4},{7,5},{8,10},{9,11},{10,... | collective-permute-start | bytes 1081352 | tf_op jit(solution)/shard_map/ppermute | solution.py:213
  39.4 2.4 %all-to-all-done.first = bf16[8,32,128]{2,1,0:T(8,128)(2,1)S(1)} async-done(((bf16[8,32,128]{2,1,0:T(8,128)(2,1)}), bf16[8,32,128]{2,1,0:T(8,128)(2,1)S(1)}, u32[]{:S(2)}, u32[]{:S(2)}) %all-to-all-start) | async-done | bytes 65568 | tf_op jit(solution)/shard_map/all_to_all | solution.py:284
  41.8 22.5 %all_to_all.10.second = bf16[16,32,128]{2,1,0:T(8,128)(2,1)S(1)} all-to-all(bf16[16,32,128]{2,1,0:T(8,128)(2,1)S(1)} %sum_near.1), channel_id=1, replica_groups=mesh['y'=8,'zh'=4,'x'=4,'zl'=2,'core'=2] {'zh','x'}, dimensions={0} | all-to-all | bytes 262144 | tf_op jit(solution)/shard_map/all_to_all | solution.py:292
  64.3 0.0 collective-permute-done.4.last
  64.3 0.8 %add_far.1 = (bf16[44,4096]{1,0:T(8,128)(2,1)}, f32[1,4096]{1,0:T(1,128)}) custom-call(f32[48,4096]{1,0:T(8,128)S(1)} %get-tuple-element.23.mine, bf16[44,4096]{1,0:T(8,128)(2,1)S(1)} %collective-permute-done.4.last, bf16[16,32,128]{2,1,0:T(8,128)(2,1)S(1)} %all_to_all.10.second), custom_call_target="tpu_custom_call" | custom-call | tf_op jit(solution)/shard_map/add_far/pallas_call | solution.py:219
  (1 shorter events, 0.0 us)
Async XLA Ops:
  0.6 13.6 %collective-permute-start = (bf16[44,4096]{1,0:T(8,128)(2,1)}, bf16[44,4096]{1,0:T(8,128)(2,1)S(1)}, u32[]{:S(2)}, u32[]{:S(2)}) collective-permute-start(bf16[44,4096]{1,0:T(8,128)(2,1)} %own.1), channel_id=1, source_target_pairs={{0,2},{1,3},{2,0},{3,1},{4,6},{5,7},{6,4},{7,5},{8,10},{9,11},{10,... | collective-permute-start | bytes 1081352 | tf_op jit(solution)/shard_map/ppermute | solution.py:213
  4.9 11.2 %collective-permute-start.1 = (bf16[44,4096]{1,0:T(8,128)(2,1)}, bf16[44,4096]{1,0:T(8,128)(2,1)S(1)}, u32[]{:S(2)}, u32[]{:S(2)}) collective-permute-start(bf16[44,4096]{1,0:T(8,128)(2,1)} %own.1), channel_id=1, source_target_pairs={{0,1},{1,0},{2,3},{3,2},{4,5},{5,4},{6,7},{7,6},{8,9},{9,8},{10,11... | collective-permute-start | bytes 1081352 | tf_op jit(solution)/shard_map/ppermute | solution.py:213
  6.8 1.4 %copy-start = (bf16[1,176,4096]{2,1,0:T(8,128)(2,1)S(1)}, bf16[1,176,4096]{2,1,0:T(8,128)(2,1)}, u32[]{:S(2)}) copy-start(bf16[1,176,4096]{2,1,0:T(8,128)(2,1)} %keys.3) | copy-start | bytes 4325380
  8.2 1.4 %copy-start.2 = (bf16[1,176,4096]{2,1,0:T(8,128)(2,1)S(1)}, bf16[1,176,4096]{2,1,0:T(8,128)(2,1)}, u32[]{:S(2)}) copy-start(bf16[1,176,4096]{2,1,0:T(8,128)(2,1)} %cot.3) | copy-start | bytes 4325380
  9.6 1.0 %copy-start.4 = (bf16[44,4096]{1,0:T(8,128)(2,1)S(1)}, bf16[44,4096]{1,0:T(8,128)(2,1)}, u32[]{:S(2)}) copy-start(bf16[44,4096]{1,0:T(8,128)(2,1)} %own.1) | copy-start | bytes 1081348
  10.6 0.7 %copy-start.5 = (f32[1,4096]{1,0:T(1,128)S(1)}, f32[1,4096]{1,0:T(1,128)}, u32[]{:S(2)}) copy-start(f32[1,4096]{1,0:T(1,128)} %gain_ref.1) | copy-start | bytes 49156
  11.3 6.5 %copy-start.3 = (bf16[1,176,4096]{2,1,0:T(8,128)(2,1)S(1)}, bf16[1,176,4096]{2,1,0:T(8,128)(2,1)}, u32[]{:S(2)}) copy-start(bf16[1,176,4096]{2,1,0:T(8,128)(2,1)} %cot.3) | copy-start | bytes 4325380
  12.1 5.7 %copy-start.1 = (bf16[1,176,4096]{2,1,0:T(8,128)(2,1)S(1)}, bf16[1,176,4096]{2,1,0:T(8,128)(2,1)}, u32[]{:S(2)}) copy-start(bf16[1,176,4096]{2,1,0:T(8,128)(2,1)} %keys.3) | copy-start | bytes 4325380
  12.1 5.7 %copy-start.6 = (f32[1,4096]{1,0:T(1,128)S(1)}, f32[1,4096]{1,0:T(1,128)}, u32[]{:S(2)}) copy-start(f32[1,4096]{1,0:T(1,128)} %gain_ref.1) | copy-start | bytes 49156
  14.2 3.6 %collective-permute-start.2 = (bf16[44,4096]{1,0:T(8,128)(2,1)S(1)}, bf16[44,4096]{1,0:T(8,128)(2,1)S(1)}, u32[]{:S(2)}, u32[]{:S(2)}) collective-permute-start(bf16[44,4096]{1,0:T(8,128)(2,1)S(1)} %collective-permute-done.far), channel_id=1, source_target_pairs={{0,1},{1,0},{2,3},{3,2},{4,5},{5,4},{6,7},{7,6},{8,9},{9,8},{10,11... | collective-permute-start | bytes 1081352 | tf_op jit(solution)/shard_map/ppermute | solution.py:213
  25.4 9.5 %collective-permute-start.3 = (bf16[96,4096]{1,0:T(8,128)(2,1)S(1)}, bf16[96,4096]{1,0:T(8,128)(2,1)S(1)}, u32[]{:S(2)}, u32[]{:S(2)}) collective-permute-start(bf16[96,4096]{1,0:T(8,128)(2,1)S(1)} %get-tuple-element.22), channel_id=1, source_target_pairs={{0,1},{1,0},{2,3},{3,2},{4,5},{5,4},{6,7},{7,6},{8,9},{9,8},{10,11... | collective-permute-start | bytes 2359304 | tf_op jit(solution)/shard_map/ppermute | solution.py:213
  27.3 14.5 %all-to-all-start = ((bf16[8,32,128]{2,1,0:T(8,128)(2,1)}), bf16[8,32,128]{2,1,0:T(8,128)(2,1)S(1)}, u32[]{:S(2)}, u32[]{:S(2)}) async-start(bf16[8,32,128]{2,1,0:T(8,128)(2,1)} %get-tuple-element.25), calls=%async_computation | async-start | bytes 131072 | tf_op jit(solution)/shard_map/all_to_all | solution.py:284
  35.7 28.6 %collective-permute-start.4 = (bf16[44,4096]{1,0:T(8,128)(2,1)}, bf16[44,4096]{1,0:T(8,128)(2,1)S(1)}, u32[]{:S(2)}, u32[]{:S(2)}) collective-permute-start(bf16[44,4096]{1,0:T(8,128)(2,1)} %get-tuple-element.24), channel_id=1, source_target_pairs={{0,2},{1,3},{2,0},{3,1},{4,6},{5,7},{6,4},{7,5},{8,10},{9,11},{10,... | collective-permute-start | bytes 1081352 | tf_op jit(solution)/shard_map/ppermute | solution.py:213

commit v7 on v6

--- a/solution.py
+++ b/solution.py
@@ -85,8 +85,8 @@
     far_rows(zl, c, far, x_ref, rs_ref, True)
 
 
-def attention_kernel(peers, near, near_rs, farcore, keys, cot, gain_ref, gk_ref, give_ref, keep_ref, gterm_ref, xf, rs,
-                     w, macc, gsum, bias0, bias1, gk, gsems):
+def attention_kernel(peers, near, near_rs, farcore, keys, cot, gain_ref, gk_ref, give_ref, keep_ref, gterm_hbm, xf, rs,
+                     gterm_ref, gterm_sem, w, macc, gsum, bias0, bias1, gk, gsems):
     part = farcore.shape[0]
     length, width = xf.shape
     zl = lax.axis_index("zl")
@@ -163,6 +163,8 @@
                 mean = None
     for i in range(peers):
         gterm_ref[i] = gsum[...].astype(BF)
+    send_gterm = pltpu.make_async_copy(gterm_ref, gterm_hbm, gterm_sem.at[0])
+    send_gterm.start()
     r = rs[...]
     m = jnp.sum(macc[...], axis=-1, keepdims=True) * (1.0 / width)
     macc[...] = r * r * m
@@ -184,6 +186,7 @@
 
     for i in range(NH // SENT):
         send_group(i).wait()
+    send_gterm.wait()
 
 
 def spread_kernel(peers, first, wide_ref):
@@ -263,9 +266,11 @@
         ),
         (x_near, rs_near, farcore, keys, grad_out, gains),
         "attention_backward",
-        hbm_out=(0,),
+        hbm_out=(0, 3),
         alias={0: 4, 1: 5},
         scratch=[
+            pltpu.VMEM((near, NH, HEAD_DIM), BF),
+            pltpu.SemaphoreType.DMA((1,)),
             pltpu.VMEM((length, width), F32),
             pltpu.VMEM((length, HEAD_DIM), F32),
             pltpu.VMEM((NH, HEAD_DIM), F32),

time: 65.7 us -> 65 us (0.989)
  no operation moved by 1% of the time
where the time goes in v7:
time: 65 us; the launch traced here: 64.5 us
  blocking collectives  22.5 us (35%)
  starting transfers between devices  21.2 us (33%)
  Pallas kernels  10.1 us (16%)
  waiting for transfers between devices  5.51 us (8%)
  local copies, waits for them, and re-layouts  4.44 us (7%)
  between operations  0.72 us (1%)
    all_to_all x1, blocking collectives, on_device(): second = lax.all_to_all(wide, ('zh', 'x'), 0, 0, tiled=True)  22.5 us
    ppermute x5, starting transfers between devices, swap(): return lax.ppermute(v, HEAD, [(i, i ^ bit) for i in range(4)])  13.7 us
    pallas_call x6, Pallas kernels, call(): pl.pallas_call(kernel, out_shape=outs, in_specs=[hbm if i in hbm_in else...  10.1 us
    all_to_all x1, starting transfers between devices, on_device(): first = lax.all_to_all(gterm, 'y', 0, 0, tiled=True)  7.57 us
    unnamed x14, local copies, waits for them, and re-layouts  4.44 us
    ppermute x5, waiting for transfers between devices, swap(): return lax.ppermute(v, HEAD, [(i, i ^ bit) for i in range(4)])  3.09 us
    all_to_all x1, waiting for transfers between devices, on_device(): first = lax.all_to_all(gterm, 'y', 0, 0, tiled=True)  2.42 us
  transfers between devices with their start and end apart: 6, of which 3 were waited for; matrix products, arithmetic and copies ran while one was open for 0% of the time, Pallas kernels for 4%

profile of v7, /device:TPU:8, one launch (start us, length us, event | category | flops | bytes accessed | tf_op | source)
XLA Modules:
  0.0 64.5 jit_solution(12208336455439383780)
XLA Ops:
  0.6 4.3 %collective-permute-start = (bf16[44,4096]{1,0:T(8,128)(2,1)}, bf16[44,4096]{1,0:T(8,128)(2,1)S(1)}, u32[]{:S(2)}, u32[]{:S(2)}) collective-permute-start(bf16[44,4096]{1,0:T(8,128)(2,1)} %own.1), channel_id=1, source_target_pairs={{0,2},{1,3},{2,0},{3,1},{4,6},{5,7},{6,4},{7,5},{8,10},{9,11},{10,... | collective-permute-start | bytes 1081352 | tf_op jit(solution)/shard_map/ppermute | solution.py:216
  4.9 1.9 %collective-permute-start.1 = (bf16[44,4096]{1,0:T(8,128)(2,1)}, bf16[44,4096]{1,0:T(8,128)(2,1)S(1)}, u32[]{:S(2)}, u32[]{:S(2)}) collective-permute-start(bf16[44,4096]{1,0:T(8,128)(2,1)} %own.1), channel_id=1, source_target_pairs={{0,1},{1,0},{2,3},{3,2},{4,5},{5,4},{6,7},{7,6},{8,9},{9,8},{10,11... | collective-permute-start | bytes 1081352 | tf_op jit(solution)/shard_map/ppermute | solution.py:216
  6.8 0.0 copy-start
  6.9 1.4 %copy-done = bf16[1,176,4096]{2,1,0:T(8,128)(2,1)S(1)} copy-done((bf16[1,176,4096]{2,1,0:T(8,128)(2,1)S(1)}, bf16[1,176,4096]{2,1,0:T(8,128)(2,1)}, u32[]{:S(2)}) %copy-start) | copy-done | bytes 1441816
  8.2 0.0 copy-start.2
  8.2 1.4 %copy-done.2 = bf16[1,176,4096]{2,1,0:T(8,128)(2,1)S(1)} copy-done((bf16[1,176,4096]{2,1,0:T(8,128)(2,1)S(1)}, bf16[1,176,4096]{2,1,0:T(8,128)(2,1)}, u32[]{:S(2)}) %copy-start.2) | copy-done | bytes 1441816
  9.6 0.0 copy-start.4
  9.6 1.0 %copy-done.4 = bf16[44,4096]{1,0:T(8,128)(2,1)S(1)} copy-done((bf16[44,4096]{1,0:T(8,128)(2,1)S(1)}, bf16[44,4096]{1,0:T(8,128)(2,1)}, u32[]{:S(2)}) %copy-start.4) | copy-done | bytes 360472
  10.6 0.0 copy-start.5
  10.6 0.7 %copy-done.5 = f32[1,4096]{1,0:T(1,128)S(1)} copy-done((f32[1,4096]{1,0:T(1,128)S(1)}, f32[1,4096]{1,0:T(1,128)}, u32[]{:S(2)}) %copy-start.5) | copy-done | bytes 16408
  11.3 0.0 copy-start.3
  11.3 0.8 %own_rows.1 = (f32[44,4096]{1,0:T(8,128)S(1)}, f32[44,128]{1,0:T(8,128)}) custom-call(bf16[44,4096]{1,0:T(8,128)(2,1)S(1)} %copy-done.4, bf16[1,176,4096]{2,1,0:T(8,128)(2,1)S(1)} %copy-done, bf16[1,176,4096]{2,1,0:T(8,128)(2,1)S(1)} %copy-done.2, f32[1,4096]{1,0:T(1,128)S(1)} %copy-done.5), custom_call_target="tpu_custom_call" | custom-call | bytes 8388608 | tf_op jit(solution)/shard_map/own_rows/pallas_call | solution.py:222
  12.1 0.0 copy-start.1
  12.1 0.0 copy-start.6
  12.1 2.1 %collective-permute-done.far = bf16[44,4096]{1,0:T(8,128)(2,1)S(1)} collective-permute-done((bf16[44,4096]{1,0:T(8,128)(2,1)}, bf16[44,4096]{1,0:T(8,128)(2,1)S(1)}, u32[]{:S(2)}, u32[]{:S(2)}) %collective-permute-start) | collective-permute-done | bytes 360480 | tf_op jit(solution)/shard_map/ppermute | solution.py:216
  14.2 1.9 %collective-permute-start.2 = (bf16[44,4096]{1,0:T(8,128)(2,1)S(1)}, bf16[44,4096]{1,0:T(8,128)(2,1)S(1)}, u32[]{:S(2)}, u32[]{:S(2)}) collective-permute-start(bf16[44,4096]{1,0:T(8,128)(2,1)S(1)} %collective-permute-done.far), channel_id=1, source_target_pairs={{0,1},{1,0},{2,3},{3,2},{4,5},{5,4},{6,7},{7,6},{8,9},{9,8},{10,11... | collective-permute-start | bytes 1081352 | tf_op jit(solution)/shard_map/ppermute | solution.py:216
  16.1 0.0 collective-permute-done.1.core
  16.2 0.7 %near_rows.1 = (f32[176,4096]{1,0:T(8,128)S(1)}, f32[176,128]{1,0:T(8,128)S(1)}) custom-call(f32[44,4096]{1,0:T(8,128)S(1)} %get-tuple-element.17.own, bf16[44,4096]{1,0:T(8,128)(2,1)S(1)} %collective-permute-done.1.core, bf16[44,4096]{1,0:T(8,128)(2,1)S(1)} %collective-permute-done.far), custom_call_target="tpu_custom_call" | custom-call | tf_op jit(solution)/shard_map/near_rows/pallas_call | solution.py:222
  16.8 1.0 %collective-permute-done.2.farcore = bf16[44,4096]{1,0:T(8,128)(2,1)S(1)} collective-permute-done((bf16[44,4096]{1,0:T(8,128)(2,1)S(1)}, bf16[44,4096]{1,0:T(8,128)(2,1)S(1)}, u32[]{:S(2)}, u32[]{:S(2)}) %collective-permute-start.2) | collective-permute-done | bytes 360480 | tf_op jit(solution)/shard_map/ppermute | solution.py:216
  17.8 0.0 copy-done.3
  17.8 0.0 copy-done.1
  17.8 0.0 copy-done.6
  17.8 6.9 %attention_backward.1 = (bf16[1,176,4096]{2,1,0:T(8,128)(2,1)}, bf16[96,4096]{1,0:T(8,128)(2,1)S(1)}, f32[96,4096]{1,0:T(8,128)S(1)}, bf16[8,32,128]{2,1,0:T(8,1...) custom-call(f32[176,4096]{1,0:T(8,128)S(1)} %get-tuple-element.19.near, ...), custom_call_target="tpu_custom_call", output_to_operand_aliasing={{4}: (0, {}), {5}: (1, {})} | custom-call | flops 1268776960 | bytes 16777216 | tf_op jit(solution)/shard_map/attention_backward/pallas_call | solution.py:222
  24.7 1.9 %collective-permute-start.3 = (bf16[96,4096]{1,0:T(8,128)(2,1)S(1)}, bf16[96,4096]{1,0:T(8,128)(2,1)S(1)}, u32[]{:S(2)}, u32[]{:S(2)}) collective-permute-start(bf16[96,4096]{1,0:T(8,128)(2,1)S(1)} %get-tuple-element.22), channel_id=1, source_target_pairs={{0,1},{1,0},{2,3},{3,2},{4,5},{5,4},{6,7},{7,6},{8,9},{9,8},{10,11... | collective-permute-start | bytes 2359304 | tf_op jit(solution)/shard_map/ppermute | solution.py:216
  26.7 7.6 %all-to-all-start = ((bf16[8,32,128]{2,1,0:T(8,128)(2,1)}), bf16[8,32,128]{2,1,0:T(8,128)(2,1)S(1)}, u32[]{:S(2)}, u32[]{:S(2)}) async-start(bf16[8,32,128]{2,1,0:T(8,128)(2,1)} %get-tuple-element.25), calls=%async_computation | async-start | bytes 131072 | tf_op jit(solution)/shard_map/all_to_all | solution.py:289
  34.2 0.0 collective-permute-done.3.got
  34.2 0.9 %add_core.1 = (f32[48,4096]{1,0:T(8,128)S(1)}, bf16[44,4096]{1,0:T(8,128)(2,1)}) custom-call(f32[96,4096]{1,0:T(8,128)S(1)} %get-tuple-element.21.keep, bf16[96,4096]{1,0:T(8,128)(2,1)S(1)} %collective-permute-done.3.got), custom_call_target="tpu_custom_call" | custom-call | tf_op jit(solution)/shard_map/add_core/pallas_call | solution.py:222
  35.1 3.6 %collective-permute-start.4 = (bf16[44,4096]{1,0:T(8,128)(2,1)}, bf16[44,4096]{1,0:T(8,128)(2,1)S(1)}, u32[]{:S(2)}, u32[]{:S(2)}) collective-permute-start(bf16[44,4096]{1,0:T(8,128)(2,1)} %get-tuple-element.24), channel_id=1, source_target_pairs={{0,2},{1,3},{2,0},{3,1},{4,6},{5,7},{6,4},{7,5},{8,10},{9,11},{10,... | collective-permute-start | bytes 1081352 | tf_op jit(solution)/shard_map/ppermute | solution.py:216
  38.7 2.4 %all-to-all-done.first = bf16[8,32,128]{2,1,0:T(8,128)(2,1)S(1)} async-done(((bf16[8,32,128]{2,1,0:T(8,128)(2,1)}), bf16[8,32,128]{2,1,0:T(8,128)(2,1)S(1)}, u32[]{:S(2)}, u32[]{:S(2)}) %all-to-all-start) | async-done | bytes 65568 | tf_op jit(solution)/shard_map/all_to_all | solution.py:289
  41.2 22.5 %all_to_all.10.second = bf16[16,32,128]{2,1,0:T(8,128)(2,1)S(1)} all-to-all(bf16[16,32,128]{2,1,0:T(8,128)(2,1)S(1)} %sum_near.1), channel_id=1, replica_groups=mesh['y'=8,'zh'=4,'x'=4,'zl'=2,'core'=2] {'zh','x'}, dimensions={0} | all-to-all | bytes 262144 | tf_op jit(solution)/shard_map/all_to_all | solution.py:297
  63.7 0.0 collective-permute-done.4.last
  63.7 0.8 %add_far.1 = (bf16[44,4096]{1,0:T(8,128)(2,1)}, f32[1,4096]{1,0:T(1,128)}) custom-call(f32[48,4096]{1,0:T(8,128)S(1)} %get-tuple-element.23.mine, bf16[44,4096]{1,0:T(8,128)(2,1)S(1)} %collective-permute-done.4.last, bf16[16,32,128]{2,1,0:T(8,128)(2,1)S(1)} %all_to_all.10.second), custom_call_target="tpu_custom_call" | custom-call | tf_op jit(solution)/shard_map/add_far/pallas_call | solution.py:222
  (1 shorter events, 0.0 us)
Async XLA Ops:
  0.6 13.6 %collective-permute-start = (bf16[44,4096]{1,0:T(8,128)(2,1)}, bf16[44,4096]{1,0:T(8,128)(2,1)S(1)}, u32[]{:S(2)}, u32[]{:S(2)}) collective-permute-start(bf16[44,4096]{1,0:T(8,128)(2,1)} %own.1), channel_id=1, source_target_pairs={{0,2},{1,3},{2,0},{3,1},{4,6},{5,7},{6,4},{7,5},{8,10},{9,11},{10,... | collective-permute-start | bytes 1081352 | tf_op jit(solution)/shard_map/ppermute | solution.py:216
  4.9 11.2 %collective-permute-start.1 = (bf16[44,4096]{1,0:T(8,128)(2,1)}, bf16[44,4096]{1,0:T(8,128)(2,1)S(1)}, u32[]{:S(2)}, u32[]{:S(2)}) collective-permute-start(bf16[44,4096]{1,0:T(8,128)(2,1)} %own.1), channel_id=1, source_target_pairs={{0,1},{1,0},{2,3},{3,2},{4,5},{5,4},{6,7},{7,6},{8,9},{9,8},{10,11... | collective-permute-start | bytes 1081352 | tf_op jit(solution)/shard_map/ppermute | solution.py:216
  6.8 1.4 %copy-start = (bf16[1,176,4096]{2,1,0:T(8,128)(2,1)S(1)}, bf16[1,176,4096]{2,1,0:T(8,128)(2,1)}, u32[]{:S(2)}) copy-start(bf16[1,176,4096]{2,1,0:T(8,128)(2,1)} %keys.3) | copy-start | bytes 4325380
  8.2 1.4 %copy-start.2 = (bf16[1,176,4096]{2,1,0:T(8,128)(2,1)S(1)}, bf16[1,176,4096]{2,1,0:T(8,128)(2,1)}, u32[]{:S(2)}) copy-start(bf16[1,176,4096]{2,1,0:T(8,128)(2,1)} %cot.3) | copy-start | bytes 4325380
  9.6 1.0 %copy-start.4 = (bf16[44,4096]{1,0:T(8,128)(2,1)S(1)}, bf16[44,4096]{1,0:T(8,128)(2,1)}, u32[]{:S(2)}) copy-start(bf16[44,4096]{1,0:T(8,128)(2,1)} %own.1) | copy-start | bytes 1081348
  10.6 0.7 %copy-start.5 = (f32[1,4096]{1,0:T(1,128)S(1)}, f32[1,4096]{1,0:T(1,128)}, u32[]{:S(2)}) copy-start(f32[1,4096]{1,0:T(1,128)} %gain_ref.1) | copy-start | bytes 49156
  11.3 6.5 %copy-start.3 = (bf16[1,176,4096]{2,1,0:T(8,128)(2,1)S(1)}, bf16[1,176,4096]{2,1,0:T(8,128)(2,1)}, u32[]{:S(2)}) copy-start(bf16[1,176,4096]{2,1,0:T(8,128)(2,1)} %cot.3) | copy-start | bytes 4325380
  12.1 5.7 %copy-start.1 = (bf16[1,176,4096]{2,1,0:T(8,128)(2,1)S(1)}, bf16[1,176,4096]{2,1,0:T(8,128)(2,1)}, u32[]{:S(2)}) copy-start(bf16[1,176,4096]{2,1,0:T(8,128)(2,1)} %keys.3) | copy-start | bytes 4325380
  12.1 5.7 %copy-start.6 = (f32[1,4096]{1,0:T(1,128)S(1)}, f32[1,4096]{1,0:T(1,128)}, u32[]{:S(2)}) copy-start(f32[1,4096]{1,0:T(1,128)} %gain_ref.1) | copy-start | bytes 49156
  14.2 3.6 %collective-permute-start.2 = (bf16[44,4096]{1,0:T(8,128)(2,1)S(1)}, bf16[44,4096]{1,0:T(8,128)(2,1)S(1)}, u32[]{:S(2)}, u32[]{:S(2)}) collective-permute-start(bf16[44,4096]{1,0:T(8,128)(2,1)S(1)} %collective-permute-done.far), channel_id=1, source_target_pairs={{0,1},{1,0},{2,3},{3,2},{4,5},{5,4},{6,7},{7,6},{8,9},{9,8},{10,11... | collective-permute-start | bytes 1081352 | tf_op jit(solution)/shard_map/ppermute | solution.py:216
  24.7 9.5 %collective-permute-start.3 = (bf16[96,4096]{1,0:T(8,128)(2,1)S(1)}, bf16[96,4096]{1,0:T(8,128)(2,1)S(1)}, u32[]{:S(2)}, u32[]{:S(2)}) collective-permute-start(bf16[96,4096]{1,0:T(8,128)(2,1)S(1)} %get-tuple-element.22), channel_id=1, source_target_pairs={{0,1},{1,0},{2,3},{3,2},{4,5},{5,4},{6,7},{7,6},{8,9},{9,8},{10,11... | collective-permute-start | bytes 2359304 | tf_op jit(solution)/shard_map/ppermute | solution.py:216
  26.7 14.5 %all-to-all-start = ((bf16[8,32,128]{2,1,0:T(8,128)(2,1)}), bf16[8,32,128]{2,1,0:T(8,128)(2,1)S(1)}, u32[]{:S(2)}, u32[]{:S(2)}) async-start(bf16[8,32,128]{2,1,0:T(8,128)(2,1)} %get-tuple-element.25), calls=%async_computation | async-start | bytes 131072 | tf_op jit(solution)/shard_map/all_to_all | solution.py:289
  35.1 28.6 %collective-permute-start.4 = (bf16[44,4096]{1,0:T(8,128)(2,1)}, bf16[44,4096]{1,0:T(8,128)(2,1)S(1)}, u32[]{:S(2)}, u32[]{:S(2)}) collective-permute-start(bf16[44,4096]{1,0:T(8,128)(2,1)} %get-tuple-element.24), channel_id=1, source_target_pairs={{0,2},{1,3},{2,0},{3,1},{4,6},{5,7},{6,4},{7,5},{8,10},{9,11},{10,... | collective-permute-start | bytes 1081352 | tf_op jit(solution)/shard_map/ppermute | solution.py:216
